TPU v7x, 256 devices: a whole 4x4x8 slice. The times are simulated.
256 devices in a mesh: outer: 16 (over y, x_hi, core), inner: 16 (over x_lo, z).
Axes of the slice: x: 4 (x_hi: 2, x_lo: 2; x = x_hi * 2 + x_lo), y: 4, z: 8, core: 2. Of those that a mesh axis runs over, the one named last changes fastest.
Arguments:
- residual_in: bfloat16 [65536, 3200], P(('outer', 'inner')), may hold values from -6 to 6
- queries: bfloat16 [65536, 1664], P(('outer', 'inner')), may hold values from -80 to 80
- keys: bfloat16 [65536, 1664], P(('outer', 'inner')), may hold values from -4.5 to 4.5
- values: bfloat16 [65536, 1664], P(('outer', 'inner')), may hold values from -12 to 12
- segment_ids: int32 [256, 256], P(('outer', 'inner')), may hold values from 0 to 7, never falling along the last dimension, each value on 1 to 128 neighbouring positions
- weight_codes: bfloat16 [3200, 1664], P('inner'), may hold values from -15 to 15, as said below
- weight_exponents: int32 [3200, 52], P('inner'), may hold values from -10 to -7
- out_grad: bfloat16 [65536, 3200], P(('outer', 'inner')), may hold values from -24 to 24
Outputs:
- layer_out: bfloat16 [65536, 3200], P(('outer', 'inner'))
- query_grad: bfloat16 [65536, 1664], P(('outer', 'inner'))
- key_grad: bfloat16 [65536, 1664], P(('outer', 'inner'))
- value_grad: bfloat16 [65536, 1664], P(('outer', 'inner'))
- weight_grad: float32 [3200, 1664], P('inner', 'outer')
Inputs may be any that keep to these rules, and one draw needn't show every extreme that they name: `weight_codes`: signed codes with four significant bits, magnitudes from 1/4 to 15.
All inputs are finite; a program needn't handle non-finite values.
Results may differ from a plain program's by a relative error of at most 0.025.
Values may be sent and summed in bfloat16 or wider, within the bound.
A program may use at most 128 MiB of HBM per device.

v0:
```python
import math

import jax
import jax.numpy as jnp
from jax import lax
from jax.sharding import PartitionSpec as P

HEADS = 13


def power_of_two(exponents):
    total = jnp.zeros(exponents.shape, jnp.float32)
    for octave in range(-16, 1):
        total = total + jnp.where(exponents == octave, 2.0**octave, 0.0)
    return total


def dequantize(codes, exponents):
    scales = jnp.repeat(power_of_two(exponents), codes.shape[1] // exponents.shape[1], axis=1)
    return (codes.astype(jnp.float32) * scales).astype(jnp.bfloat16)


def heads_first(array):
    return array.reshape(array.shape[0], HEADS, array.shape[1] // HEADS).transpose(1, 0, 2)


def heads_last(array):
    return array.transpose(1, 0, 2).reshape(array.shape[1], array.shape[0] * array.shape[2])


def head_probs(query, key_rows, same):
    scores = lax.dot_general(
        query, key_rows, (((1,), (1,)), ((), ())), preferred_element_type=jnp.float32
    )
    scores = scores * (1.0 / math.sqrt(query.shape[1]))
    return jax.nn.softmax(jnp.where(same, scores, -jnp.inf), axis=-1)


def pack_forward(queries, keys, values, segments):
    same = segments[:, None] == segments[None, :]

    def one_head(triple):
        query, key_rows, value_rows = triple
        rounded = head_probs(query, key_rows, same).astype(jnp.bfloat16)
        return jnp.dot(rounded, value_rows, preferred_element_type=jnp.float32).astype(jnp.bfloat16)

    return heads_last(
        lax.map(one_head, (heads_first(queries), heads_first(keys), heads_first(values)))
    )


def pack_backward(queries, keys, values, segments, attended, attended_grad):
    same = segments[:, None] == segments[None, :]

    def one_head(group):
        query, key_rows, value_rows, output, output_grad = group
        probs = head_probs(query, key_rows, same)
        rounded = probs.astype(jnp.bfloat16)
        value_grad = lax.dot_general(
            rounded, output_grad, (((0,), (0,)), ((), ())), preferred_element_type=jnp.float32
        ).astype(jnp.bfloat16)
        prob_grad = lax.dot_general(
            output_grad, value_rows, (((1,), (1,)), ((), ())), preferred_element_type=jnp.float32
        )
        delta = jnp.sum(
            output_grad.astype(jnp.float32) * output.astype(jnp.float32), axis=1, keepdims=True
        )
        score_grad = (probs * (prob_grad - delta)).astype(jnp.bfloat16)
        factor = 1.0 / math.sqrt(query.shape[1])
        query_grad = (
            jnp.dot(score_grad, key_rows, preferred_element_type=jnp.float32) * factor
        ).astype(jnp.bfloat16)
        key_grad = (
            lax.dot_general(
                score_grad, query, (((0,), (0,)), ((), ())), preferred_element_type=jnp.float32
            )
            * factor
        ).astype(jnp.bfloat16)
        return (query_grad, key_grad, value_grad)

    stacked = lax.map(
        one_head,
        (
            heads_first(queries),
            heads_first(keys),
            heads_first(values),
            heads_first(attended),
            heads_first(attended_grad),
        ),
    )
    return tuple((heads_last(member) for member in stacked))


def body(residual_in, queries, keys, values, segment_ids, weight_codes, weight_exponents, out_grad):
    weight_part = dequantize(weight_codes, weight_exponents)
    segments = segment_ids[0]
    attended = pack_forward(queries, keys, values, segments)
    projected = lax.dot_general(
        attended,
        lax.all_gather(weight_part, "inner", axis=0, tiled=True),
        (((1,), (1,)), ((), ())),
        preferred_element_type=jnp.float32,
    )
    columns = out_grad
    attended_grad = jnp.dot(
        columns,
        lax.all_gather(weight_part, "inner", axis=0, tiled=True),
        preferred_element_type=jnp.float32,
    ).astype(jnp.bfloat16)
    layer_out = (residual_in.astype(jnp.float32) + projected).astype(jnp.bfloat16)
    columns = out_grad
    row_share = lax.psum_scatter(
        lax.dot_general(
            columns, attended, (((0,), (0,)), ((), ())), preferred_element_type=jnp.float32
        ).astype(jnp.bfloat16),
        "inner",
        scatter_dimension=0,
        tiled=True,
    )
    summed = lax.psum_scatter(row_share, "outer", scatter_dimension=1, tiled=True).astype(
        jnp.float32
    )
    tokens_all = out_grad.shape[0] * lax.axis_size("outer") * lax.axis_size("inner")
    weight_grad = summed * (1.0 / math.sqrt(tokens_all))
    query_grad, key_grad, value_grad = pack_backward(
        queries, keys, values, segments, attended, attended_grad
    )
    return (layer_out, query_grad, key_grad, value_grad, weight_grad)


def solution(mesh):
    in_specs = (
        P(("outer", "inner"), None),
        P(("outer", "inner"), None),
        P(("outer", "inner"), None),
        P(("outer", "inner"), None),
        P(("outer", "inner"), None),
        P("inner", None),
        P("inner", None),
        P(("outer", "inner"), None),
    )
    out_specs = (
        P(("outer", "inner"), None),
        P(("outer", "inner"), None),
        P(("outer", "inner"), None),
        P(("outer", "inner"), None),
        P("inner", "outer"),
    )
    return jax.shard_map(body, mesh=mesh, in_specs=in_specs, out_specs=out_specs, check_vma=False)
```

profile of v0, /device:TPU:1, one launch (start us, length us, event | category | flops | bytes accessed | tf_op | source)
XLA Modules:
  0.0 627.0 jit_solution(6867368413482996527)
XLA Ops:
  7.2 1.6 copy.62
  8.9 1.3 copy.65
  10.2 1.5 copy.63
  11.8 1.3 copy.66
  13.1 1.5 copy.64
  14.7 1.3 copy.67
  16.0 29.6 %while.26 = (s32[]{:T(128)}, bf16[13,256,128]{2,1,0:T(8,128)(2,1)S(1)}, bf16[13,256,128]{2,1,0:T(8,128)(2,1)}, bf16[13,256,128]{2,1,0:T(8,128)(2,1)}, bf16[13,25...) while((s32[]{:T(128)}, bf16[13,256,128]{2,1,0:T(8,128)(2,1)S(1)}, ...), condition=%wide.region_3.4_spmd.clone, body=%wide.region_0.3_spmd.clone.sunk | while | flops 34176512 | bytes 1057869 | solution.py:48
  18.3 1.1 fusion.82
  20.6 1.1 fusion.82
  22.9 1.1 fusion.82
  25.2 1.1 fusion.82
  27.4 1.1 fusion.82
  29.7 1.1 fusion.82
  32.0 1.1 fusion.82
  34.3 1.1 fusion.82
  36.6 1.1 fusion.82
  38.8 1.1 fusion.82
  41.1 1.1 fusion.82
  43.4 1.1 fusion.82
  46.3 5.5 fusion.50
  53.8 249.2 %all-reduce.3.cloned.1.call-done = bf16[3200,1664]{0,1:T(8,128)(2,1)} async-done(((bf16[3200,1664]{0,1:T(8,128)(2,1)}), bf16[3200,1664]{0,1:T(8,128)(2,1)}) %all-reduce.3.cloned.1.call-update) | async-done | bytes 10649616
  302.9 2.6 constant_dynamic-slice_fusion
  306.1 1.6 copy.69
  307.6 2.5 multiply_convert_fusion
  310.1 66.1 %reduce-scatter.3.cloned.1.call-done = bf16[200,104]{0,1:T(8,128)(2,1)} async-done(((bf16[200,1664]{0,1:T(8,128)(2,1)}), bf16[200,104]{0,1:T(8,128)(2,1)}) %reduce-scatter.3.cloned.1.call-update) | async-done | bytes 41616 | tf_op jit(solution)/shard_map/reduce_scatter | solution.py:120
  377.8 124.9 %all-gather.2.cloned.1.call-done = bf16[3200,1664]{1,0:T(8,128)(2,1)} async-done(((bf16[200,1664]{1,0:T(8,128)(2,1)}), bf16[3200,1664]{1,0:T(8,128)(2,1)}) %all-gather.2.cloned.1.call-update) | async-done | bytes 10649616 | tf_op jit(solution)/shard_map/all_gather | solution.py:100
  502.8 7.1 %convolution_convert_fusion.3 = bf16[1664,256]{1,0:T(8,128)(2,1)S(1)} fusion(bf16[3200,1664]{1,0:T(8,128)(2,1)} %all-gather.2.cloned.1.call-done, bf16[256,3200]{1,0:T(8,128)(2,1)S(1)} %copy-done), kind=kOutput, calls=%fused_computation.65 | convolution fusion | flops 2726723584 | bytes 13139968 | tf_op jit(solution)/shard_map/dot_general | solution.py:105
  510.6 92.3 %while.27 = (s32[]{:T(128)}, bf16[13,256,128]{1,2,0:T(8,128)(2,1)}, bf16[13,256,128]{1,2,0:T(8,128)(2,1)}, bf16[13,256,128]{1,2,0:T(8,128)(2,1)}, bf16[13,256,12...) while((s32[]{:T(128)}, bf16[13,256,128]{1,2,0:T(8,128)(2,1)}, ...), condition=%wide.region_8.9_spmd.clone, body=%wide.region_4.8_spmd.clone.sunk | while | flops 85097728 | bytes 3030133 | solution.py:81
  602.9 2.3 copy.77
  605.2 1.3 copy.78
  606.6 2.2 copy.79
  608.7 11.7 %fusion.51 = bf16[256,3200]{1,0:T(8,128)(2,1)} fusion(bf16[256,1664]{0,1:T(8,128)(2,1)S(1)} %bitcast.127, bf16[3200,1664]{1,0:T(8,128)(2,1)} %all-gather.2.cloned.1.call-done, bf16[256,3200]{1,0:T(8,128)(2,1)} %param.12), kind=kOutput, calls=%fused_computation.64 | convolution fusion | flops 2728755200 | bytes 14778368 | tf_op jit(solution)/shard_map/dot_general | solution.py:98
  (216 shorter events, 112.4 us)
Async XLA Ops:
  7.2 39.2 %copy-start = (bf16[256,3200]{1,0:T(8,128)(2,1)S(1)}, bf16[256,3200]{1,0:T(8,128)(2,1)}, u32[]{:S(2)}) copy-start(bf16[256,3200]{1,0:T(8,128)(2,1)} %param.19) | copy-start | bytes 4915204
  7.2 295.8 %all-reduce.3.cloned.1.call-start = ((), (), s32[]{:S(2)}) async-start(), calls=%async_computation.3 | async-start | bytes 21299200
  13.1 2.9 copy-start.6
  45.7 6.2 copy-start.3
  46.3 5.5 copy-start.1
  51.9 0.7 copy-start.7
  51.9 253.9 %copy-start.5 = (s32[200,52]{0,1:T(8,128)S(1)}, s32[200,52]{0,1:T(8,128)}, u32[]{:S(2)}) copy-start(s32[200,52]{0,1:T(8,128)} %param.18) | copy-start | bytes 124804
  51.9 324.4 %reduce-scatter.3.cloned.1.call-start = ((), (), s32[]{:S(2)}) async-start(), calls=%async_computation.2 | async-start | bytes 905216 | tf_op jit(solution)/shard_map/reduce_scatter | solution.py:120
  305.6 197.2 %all-gather.2.cloned.1.call-start = ((), (), s32[]{:S(2)}) async-start(), calls=%async_computation.1 | async-start | bytes 11315200 | tf_op jit(solution)/shard_map/all_gather | solution.py:100
  602.9 2.3 copy-start.4
  605.2 3.5 copy-start.2
Sparse Core Ops, SparseCore 0:
  52.0 250.8 all-reduce.2
  307.6 68.6 reduce-scatter.2
  378.1 124.6 all-gather.1
where the time goes:
time: 632 us; the launch traced here: 627 us
  waiting for transfers between devices  440 us (70%)
  matrix products  110 us (17%)
  local copies, waits for them, and re-layouts  43.2 us (7%)
  other arithmetic  17.8 us (3%)
  between operations  14.6 us (2%)
    unnamed x4, waiting for transfers between devices  249 us
    all_gather x1, waiting for transfers between devices, body(): lax.all_gather(weight_part, 'inner', axis=0, tiled=True)  125 us
    reduce_scatter x1, waiting for transfers between devices, body(): lax.psum_scatter(row_share, 'outer', scatter_dimension=1, tiled=True)  66.1 us
    dot_general x26, matrix products, head_probs(): lax.dot_general(query, key_rows, (((1,), (1,)), ((), ())), preferred_elem...  28.4 us
    dynamic_update_slice x65, local copies, waits for them, and re-layouts, pack_forward(): lax.map(one_head, (heads_first(queries), heads_first(keys), heads_first(v...  21.1 us
    unnamed x28, local copies, waits for them, and re-layouts  19.1 us
    dot_general x13, matrix products, one_head(): jnp.dot(rounded, value_rows, preferred_element_type=jnp.float32)  14.2 us
    dot_general x13, matrix products, one_head(): jnp.dot(score_grad, key_rows, preferred_element_type=jnp.float32) * factor  13.8 us
  transfers between devices with their start and end apart: 3, of which 3 were waited for; matrix products, arithmetic and copies ran while one was open for 1% of the time, Pallas kernels for 0%

commit v1 on v0

v1 whole, which is shorter than its diff:
```python
import functools
import math

import jax
import jax.numpy as jnp
from jax import lax
from jax.experimental import pallas as pl
from jax.experimental.pallas import tpu as pltpu
from jax.sharding import PartitionSpec as P

MESH = pl.DeviceIdType.MESH
BF = jnp.bfloat16
F32 = jnp.float32

TOK = 256
D = 3200
HD = 1664
HEADS = 13
BLOCK = 32
T = 128
RB = 200
RP = 208
SPAN = ((0, 112), (112, 96))
CARRY = 1152
SHARE = 512
TOP = (4, 3)


def chain(way, half):
    return TOP[half] if way == 0 else TOP[1 - half]


def dot(a, b, ca, cb):
    return lax.dot_general(a, b, (((ca,), (cb,)), ((), ())), preferred_element_type=F32)


def lanes(rows):
    return lax.broadcasted_iota(jnp.int32, (rows, T), 1)


def body_kernel(
    seg_ref, codes_ref, exps_ref, q_hbm, k_hbm, v_hbm, og_hbm, res_hbm,
    lo_hbm, dq_hbm, dk_hbm, dv_hbm, wg_ref,
    W, PG, YR, XR, ZR, LB, FR, SR, SS, OGR, OGS, ATR, ATT, PST, AGF, AGB, Q, K, V, OG, LO, BIAS,
    in_sem, out_sem, zs, zr, xs, xr, ys, yr, ss, sr, gys, gyr, gxs, gxr, gzs, gzr, fs, fr, cs, cr,
):
    o = lax.axis_index("outer")
    i = lax.axis_index("inner")
    y = o // 4
    xh = (o // 2) % 2
    c = o % 2
    xl = i // 8
    z = i % 8
    x = xh * 2 + xl
    par = y % 2
    is_a = c == xl
    is_b = c != xl
    own_col = pl.multiple_of(par * SHARE, T)
    give_col = pl.multiple_of(par * CARRY, T)
    take_col = pl.multiple_of((1 - par) * CARRY, T)

    def device(x_, y_, z_, c_):
        return ((y_ * 2 + x_ // 2) * 2 + c_, (x_ % 2) * 8 + z_)

    def along_x(step):
        return device((x + step + 4) % 4, y, z, c)

    def along_y(step):
        return device(x, (y + step + 4) % 4, z, c)

    def along_z(step):
        return device(x, y, (z + step + 8) % 8, c)

    sibling = device(x, y, z, 1 - c)

    def owner_device(dy, dx):
        return device((xh if dx == 0 else 1 - xh) * 2 + xl, (y + dy) % 4, z, c)

    def remote(src, dst, ssem, rsem, dev):
        return pltpu.make_async_remote_copy(
            src_ref=src, dst_ref=dst, send_sem=ssem, recv_sem=rsem, device_id=dev, device_id_type=MESH
        )

    loads = [
        pltpu.make_async_copy(src, dst, in_sem.at[n])
        for n, (src, dst) in enumerate(
            ((og_hbm, OG), (q_hbm, Q), (k_hbm, K), (v_hbm, V), (res_hbm, LO))
        )
    ]
    barrier = pltpu.get_barrier_semaphore()
    greet = [along_z(1), along_z(-1), along_x(1), along_x(-1), along_y(1), along_y(-1), sibling]
    greet += [owner_device(2, 0), owner_device(0, 1), owner_device(1, 1), owner_device(2, 1), owner_device(3, 1)]
    for dev in greet:
        pl.semaphore_signal(barrier, inc=1, device_id=dev, device_id_type=MESH)
    for load in loads:
        load.start()

    exps = exps_ref[...]
    scale = jnp.zeros(exps.shape, F32)
    for octave in range(-16, 1):
        scale = scale + jnp.where(exps == octave, 2.0**octave, 0.0)
    spread = (
        lax.broadcasted_iota(jnp.int32, (HD // BLOCK, HD), 1) // BLOCK
        == lax.broadcasted_iota(jnp.int32, (HD // BLOCK, HD), 0)
    ).astype(BF)
    wide = jnp.dot(scale.astype(BF), spread, preferred_element_type=F32)
    block = codes_ref[...].astype(F32) * wide
    block = jnp.concatenate([block, jnp.zeros((RP - RB, HD), F32)], axis=0)
    W[xl * 8 + z] = block.astype(BF)

    pl.semaphore_wait(barrier, len(greet))

    def zz(e):
        return (z + e) % 8

    def rows(half):
        return pl.ds(*SPAN[half])

    def mine(e):
        return c * 8 + zz(e)

    def theirs(e):
        return (1 - c) * 8 + zz(e)

    def z_copy(way, half, step):
        e = (9 - step) % 8 if way == 0 else step - 1
        part = W.at[mine(e), rows(half), pl.ds(own_col, CARRY)]
        return remote(part, part, zs.at[way, half, step - 1], zr.at[way, half, step - 1], along_z(1 - 2 * way))

    def z_arrival(way, half, step):
        e = 8 - step if way == 0 else step
        part = W.at[mine(e), rows(half), pl.ds(own_col, CARRY)]
        return remote(part, part, zs.at[way, half, step - 1], zr.at[way, half, step - 1], along_z(1 - 2 * way))

    def x_copy(e, half):
        part = W.at[mine(e), rows(half), pl.ds(own_col, CARRY)]
        turn = (half + min(e, 8 - e)) % 2
        return remote(part, part, xs.at[e, half], xr.at[e, half], along_x(1 - 2 * turn))

    def y_copy(e, half, way):
        part = W.at[mine(e), rows(half), pl.ds(pl.multiple_of(give_col + 256 * way, T), 256)]
        return remote(part, part, ys.at[e, half, way], yr.at[e, half, way], along_y(1 - 2 * way))

    def y_arrival(e, half, way):
        part = W.at[mine(e), rows(half), pl.ds(pl.multiple_of(take_col + 256 * way, T), 256)]
        return remote(part, part, ys.at[e, half, way], yr.at[e, half, way], along_y(1 - 2 * way))

    def s_copy(e, half, kind, at=mine):
        cols = pl.ds(own_col, CARRY) if kind == 0 else pl.ds(take_col, SHARE)
        part = W.at[at(e), rows(half), cols]
        return remote(part, part, ss.at[e, half, kind], sr.at[e, half, kind], sibling)

    def spread_out(e, half):
        for way in (0, 1):
            y_copy(e, half, way).start()
        s_copy(e, half, 0).start()

    chunks = [
        [(0, 0), (0, 1)],
        [(7, 0), (1, 0)], [(7, 1), (1, 1)], [(6, 0), (2, 0)], [(6, 1), (2, 1)],
        [(5, 0), (3, 0)], [(5, 1), (3, 1)], [(4, 0), (4, 1)],
    ]

    def serve_z(n):
        @pl.when(is_a)
        def _():
            for e, half in chunks[n]:
                way = (0 if half == 0 else 1) if e == 4 else (0 if e > 4 else 1)
                step = 8 - e if way == 0 else e
                z_arrival(way, half, step).wait_recv()
                if step < chain(way, half):
                    z_copy(way, half, step + 1).start()
                x_copy(e, half).start()
                spread_out(e, half)

    def serve_x(n):
        @pl.when(is_b)
        def _():
            for e, half in chunks[n]:
                x_copy(e, half).wait_recv()
                spread_out(e, half)

    def serve_y(n):
        def go():
            for e, half in chunks[n]:
                for way in (0, 1):
                    y_arrival(e, half, way).wait_recv()
                s_copy(e, half, 1).start()

        if n == 0:
            pl.when(is_b)(go)
        else:
            go()

    @pl.when(is_a)
    def _():
        for half in (0, 1):
            for way in (0, 1):
                z_copy(way, half, 1).start()
            x_copy(0, half).start()

    seg = jnp.broadcast_to(seg_ref[...].astype(F32), (TOK, TOK))
    BIAS[...] = jnp.where(seg == seg.T, 0.0, -1e30)
    factor = 1.0 / math.sqrt(T)

    def head_columns(h):
        return pl.ds(pl.multiple_of(h * T, T), T)

    def forward(h, carry):
        cols = head_columns(h)
        s = dot(Q[:, cols], K[:, cols], 1, 1) * factor + BIAS[...]
        s = jnp.exp(s - jnp.max(s, axis=1, keepdims=True))
        p = s * (1.0 / jnp.sum(s, axis=1, keepdims=True))
        PST[h] = p
        ATT[:, cols] = dot(p.astype(BF), V[:, cols], 1, 0).astype(BF)
        return carry

    def og_blocks(kz, carry):
        lane = lanes(TOK)
        for other in (0, 1):
            b = (c if other == 0 else 1 - c) * 8 + kz
            first = (RB * b) // T
            shift = (RB * b) % T
            back = (T - shift) % T
            tiles = [
                pltpu.roll(
                    OG[:, pl.ds(pl.multiple_of(jnp.minimum(first + n, D // T - 1) * T, T), T)].astype(F32), back, 1
                )
                for n in range(3)
            ]
            left = jnp.where(lane < T - shift, tiles[0], tiles[1]).astype(BF)
            right = jnp.where(lane < T - shift, tiles[1], tiles[2])
            right = jnp.where(lane < RB - T, right, 0.0).astype(BF)
            if other == 0:
                OGR[kz, 0:TOK, 0:T] = left
                OGR[kz, 0:TOK, T : 2 * T] = right
            else:
                OGS[kz, :, 0:T] = left
                OGS[kz, :, T : 2 * T] = right
        return carry

    og_share = remote(OGS, OGR.at[:, pl.ds(TOK, TOK), :], cs.at[0], cr.at[0], sibling)
    at_share = remote(ATR.at[pl.ds(0, TOK), :], ATR.at[pl.ds(TOK, TOK), :], cs.at[1], cr.at[1], sibling)

    pieces = []
    for j in range(8):
        pos = (j // 2 % 2) * 9 + (j // 4) * 2 + j % 2
        pieces.append((pos * T, 208 * j, T))
        pieces.append((SHARE + 80 * j, 208 * j + T, 80))

    def order_columns(n, carry):
        size = 64
        block_rows = pl.ds(pl.multiple_of(n * size, size), size)
        lane = lanes(size)
        done = {}
        for dst, src, length in pieces:
            for t in range(dst // T, (dst + length - 1) // T + 1):
                for u in range(src // T, (src + length - 1) // T + 1):
                    low = max(dst, t * T, dst + T * u - src) - t * T
                    high = min(dst + length, (t + 1) * T, dst + T * (u + 1) - src) - t * T
                    if low >= high:
                        continue
                    tile = ATT[block_rows, u * T : (u + 1) * T].astype(F32)
                    shift = (dst - src) % T
                    if shift:
                        tile = pltpu.roll(tile, shift, 1)
                    if t in done:
                        tile = jnp.where((lane >= low) & (lane < high), tile, done[t])
                    done[t] = tile
        for t, tile in done.items():
            ATR[block_rows, t * T : (t + 1) * T] = tile.astype(BF)
        return carry

    def place(n):
        return (4 + ((n + 1) // 2) * (2 * (n % 2) - 1)) % 8

    def gy_copy(e, way):
        return remote(
            PG.at[zz(e), :, pl.ds(pl.multiple_of(take_col + 256 * way, T), 256)],
            YR.at[e, :, pl.ds(256 * way, 256)],
            gys.at[e, way], gyr.at[e, way], along_y(1 - 2 * way),
        )

    def partial_product(n, carry):
        e = place(n)
        for start, size in ((0, 512), (512, 640), (1152, 512)):
            prod = dot(OGR[zz(e), :, 0:RP], ATR[:, start : start + size], 0, 0)
            PG[zz(e), :, start : start + size] = prod.astype(BF)
        for way in (0, 1):
            gy_copy(e, way).start()
        return carry

    def gx_copy(e, half):
        turn = (half + jnp.minimum(e, 8 - e)) % 2
        return remote(
            PG.at[zz(e), rows(half), pl.ds(own_col, CARRY)],
            XR.at[e, rows(half), :],
            gxs.at[e, half], gxr.at[e, half], along_x(1 - 2 * turn),
        )

    def add_y(n, carry):
        e = place(n)
        for way in (0, 1):
            gy_copy(e, way).wait_recv()
        cols = pl.ds(give_col, SHARE)
        PG[zz(e), :, cols] = (PG[zz(e), :, cols].astype(F32) + YR[e].astype(F32)).astype(BF)

        @pl.when(is_b)
        def _():
            for half in (0, 1):
                gx_copy(e, half).start()

        return carry

    def add_x(n, carry):
        @pl.when(is_a)
        def _():
            e = place(n)
            for half in (0, 1):
                gx_copy(e, half).wait_recv()
            cols = pl.ds(own_col, CARRY)
            PG[zz(e), :, cols] = (PG[zz(e), :, cols].astype(F32) + XR[e].astype(F32)).astype(BF)

        return carry

    def gz_copy(way, half, reach):
        e = reach if way == 0 else 8 - reach
        return remote(
            PG.at[zz(e), rows(half), pl.ds(own_col, CARRY)],
            ZR.at[way, reach - 1, rows(half), :],
            gzs.at[way, half, reach - 1], gzr.at[way, half, reach - 1], along_z(1 - 2 * way),
        )

    def serve_gz(reach):
        @pl.when(is_a)
        def _():
            for half in (0, 1):
                for way in (0, 1):
                    top = chain(way, half)
                    if reach > top:
                        continue
                    if reach < top:
                        gz_copy(way, half, reach + 1).wait_recv()
                        e = (reach if way == 0 else 8 - reach) % 8
                        span = rows(half)
                        cols = pl.ds(own_col, CARRY)
                        PG[zz(e), span, cols] = (
                            PG[zz(e), span, cols].astype(F32) + ZR[way, reach, span, :].astype(F32)
                        ).astype(BF)
                    if reach > 0:
                        gz_copy(way, half, reach).start()

    turns = [(dy, dx) for dy in range(4) for dx in range(2)][1:]

    def owner(dy, dx):
        return (((y + dy) % 4) * 2 + (xh if dx == 0 else 1 - xh))

    def f_copy(dy, dx):
        slot = 2 * dy + dx
        size = 256 if dy % 2 == 0 else T
        return remote(
            LB.at[owner(dy, dx), :, pl.ds(0, size)],
            FR.at[slot, :, pl.ds(0, size)],
            fs.at[slot], fr.at[slot], owner_device(dy, dx),
        )

    def send_last():
        for j in range(8):
            u, shift = divmod(80 * j, T)
            tile = PG[z, :, SHARE + u * T : SHARE + (u + 1) * T].astype(F32)
            if shift:
                tile = pltpu.roll(tile, T - shift, 1)
            if shift + 80 > T:
                more = PG[z, :, SHARE + (u + 1) * T : SHARE + (u + 2) * T].astype(F32)
                tile = jnp.where(lanes(RP) < T - shift, tile, pltpu.roll(more, T - shift, 1))
            LB[j, :, 0:T] = tile.astype(BF)
        for m in range(4):
            j = (m // 2) * 4 + m % 2 + 2 * par
            LB[j, :, T : 2 * T] = PG[z, :, pl.ds(pl.multiple_of(par * CARRY + m * T, T), T)]
        for dy, dx in turns:
            f_copy(dy, dx).start()

    share = remote(SS, SR, cs.at[2], cr.at[2], sibling)

    def finish():
        me = owner(0, 0)
        rest = LB[me, :, 0:T].astype(F32)
        main = LB[me, :, T : 2 * T].astype(F32)
        for dy, dx in turns:
            f_copy(dy, dx).wait_recv()
            rest = rest + FR[2 * dy + dx, :, 0:T].astype(F32)
            if dy % 2 == 0:
                main = main + FR[2 * dy + dx, :, T : 2 * T].astype(F32)
        norm = 1.0 / math.sqrt(TOK * 256)
        main = main * norm
        rest = rest * norm
        second = jnp.where(lanes(RP) < 24, pltpu.roll(main, 24, 1), pltpu.roll(rest, 24, 1))
        SS[...] = jnp.where(c == 0, second, main)
        share.start()
        wg_ref[...] = jnp.where(c == 0, main, second)[0:RB, 0:104]

    def grad_in(kz, carry):
        for start, size in ((0, 512), (512, 640), (1152, 512)):
            cols = pl.ds(start, size)
            AGF[:, cols] += dot(OGR[kz, 0:TOK, 0:RP], W[c * 8 + kz, :, cols], 1, 0) + dot(
                OGS[kz, :, 0:RP], W[(1 - c) * 8 + kz, :, cols], 1, 0
            )
        return carry

    def project(b, carry):
        prod = dot(ATT[...], W[b], 1, 1)
        lane = lanes(TOK)
        first = (RB * b) // T
        shift = (RB * b) % T
        one = pltpu.roll(prod[:, 0:T], shift, 1)
        tail = jnp.concatenate([prod[:, T:RP], jnp.zeros((TOK, 2 * T - RP), F32)], axis=1)
        two = pltpu.roll(tail, shift, 1)

        def put(n, mask, value):
            cols = pl.ds(pl.multiple_of(jnp.minimum(first + n, D // T - 1) * T, T), T)
            old = LO[:, cols]
            new = (old.astype(F32) + value).astype(BF)
            LO[:, cols] = jnp.where(mask, new, old)

        put(0, lane >= shift, one)
        put(1, lane - shift < RB - T, jnp.where(lane < shift, one, two))
        put(2, lane < shift - (2 * T - RB), two)
        return carry

    def backward(h, carry):
        cols = head_columns(h)
        p = PST[h]
        dout = AGB[:, cols]
        q, k, v = Q[:, cols], K[:, cols], V[:, cols]
        delta = jnp.sum(dout.astype(F32) * ATT[:, cols].astype(F32), axis=1, keepdims=True)
        ds = (p * (dot(dout, v, 1, 1) - delta)).astype(BF)
        V[:, cols] = dot(p.astype(BF), dout, 0, 0).astype(BF)
        Q[:, cols] = (dot(ds, k, 1, 0) * factor).astype(BF)
        K[:, cols] = (dot(ds, q, 0, 0) * factor).astype(BF)
        return carry

    def loop(low, high, what):
        lax.fori_loop(low, high, what, 0)

    for load in loads:
        load.wait()
    loop(0, 8, og_blocks)
    og_share.start()
    loop(0, 4, forward)
    serve_z(1)
    serve_x(0)
    loop(4, 8, forward)
    serve_z(2)
    serve_x(1)
    loop(8, 13, forward)
    loop(0, 4, order_columns)
    at_share.start()
    serve_z(3)
    serve_x(2)
    serve_y(0)
    serve_y(1)
    og_share.wait()
    at_share.wait()
    loop(0, 2, partial_product)
    serve_z(4)
    serve_x(3)
    serve_y(2)
    loop(2, 4, partial_product)
    serve_z(5)
    serve_x(4)
    serve_y(3)
    loop(4, 6, partial_product)
    serve_z(6)
    serve_x(5)
    serve_y(4)
    loop(6, 8, partial_product)
    serve_z(7)
    serve_x(6)
    serve_y(5)
    AGF[...] = jnp.zeros((TOK, HD), F32)
    loop(0, 2, add_y)
    serve_x(7)
    serve_y(6)
    loop(2, 4, add_y)
    serve_y(7)

    for n in range(8):
        for e, half in chunks[n]:
            for kind in (0, 1):
                if e == 0:
                    @pl.when(is_a)
                    def _():
                        s_copy(e, half, kind, theirs).wait_recv()
                else:
                    s_copy(e, half, kind, theirs).wait_recv()

    loop(0, 1, add_x)
    serve_gz(4)
    loop(0, 4, grad_in)
    loop(4, 5, add_y)
    loop(1, 3, add_x)
    serve_gz(3)
    loop(4, 8, grad_in)
    AGB[...] = AGF[...].astype(BF)
    loop(5, 6, add_y)
    loop(0, 4, backward)
    loop(6, 8, add_y)
    loop(3, 5, add_x)
    serve_gz(2)
    loop(4, 8, backward)
    loop(5, 7, add_x)
    serve_gz(1)
    loop(8, 13, backward)
    outs = [
        pltpu.make_async_copy(src, dst, out_sem.at[n])
        for n, (src, dst) in enumerate(((Q, dq_hbm), (K, dk_hbm), (V, dv_hbm), (LO, lo_hbm)))
    ]
    for n in range(3):
        outs[n].start()
    loop(7, 8, add_x)
    serve_gz(0)
    pl.when(is_a)(send_last)
    loop(0, 16, project)
    outs[3].start()
    pl.when(is_a)(finish)

    @pl.when(is_b)
    def _():
        share.wait_recv()
        wg_ref[...] = SR[0:RB, 0:104]

    for n in range(8):
        for e, half in chunks[n]:
            def sent(e=e, half=half):
                for way in (0, 1):
                    y_copy(e, half, way).wait_send()
                for kind in (0, 1):
                    s_copy(e, half, kind).wait_send()

            if e == 0:
                pl.when(is_b)(sent)
            else:
                sent()

    def sent_y(e, carry):
        for way in (0, 1):
            gy_copy(e, way).wait_send()
        return carry

    loop(0, 8, sent_y)

    @pl.when(is_b)
    def _():
        def sent_x(e, carry):
            for half in (0, 1):
                gx_copy(e, half).wait_send()
            return carry

        loop(0, 8, sent_x)

    @pl.when(is_a)
    def _():
        for e in range(8):
            for half in (0, 1):
                x_copy(e, half).wait_send()
        for half in (0, 1):
            for way in (0, 1):
                for step in range(1, chain(way, half) + 1):
                    z_copy(way, half, step).wait_send()
                    gz_copy(way, half, step).wait_send()
        for dy, dx in turns:
            f_copy(dy, dx).wait_send()
        share.wait_send()

    for out in outs:
        out.wait()


def block_step(residual_in, queries, keys, values, segment_ids, weight_codes, weight_exponents, out_grad):
    vmem = pl.BlockSpec(memory_space=pltpu.VMEM)
    hbm = pl.BlockSpec(memory_space=pl.ANY)
    dma = pltpu.SemaphoreType.DMA
    V = pltpu.VMEM
    layer_out, query_grad, key_grad, value_grad, weight_grad = pl.pallas_call(
        body_kernel,
        out_shape=(
            jax.ShapeDtypeStruct((TOK, D), BF),
            jax.ShapeDtypeStruct((TOK, HD), BF),
            jax.ShapeDtypeStruct((TOK, HD), BF),
            jax.ShapeDtypeStruct((TOK, HD), BF),
            jax.ShapeDtypeStruct((RB, 104), F32),
        ),
        in_specs=[vmem] * 3 + [hbm] * 5,
        out_specs=(hbm, hbm, hbm, hbm, vmem),
        scratch_shapes=[
            V((16, RP, HD), BF),
            V((8, RP, HD), BF),
            V((8, RP, SHARE), BF),
            V((8, RP, CARRY), BF),
            V((2, 4, RP, CARRY), BF),
            V((8, RP, 2 * T), BF),
            V((8, RP, 2 * T), BF),
            V((RP, T), F32),
            V((RP, T), F32),
            V((8, 2 * TOK, 2 * T), BF),
            V((8, TOK, 2 * T), BF),
            V((2 * TOK, HD), BF),
            V((TOK, HD), BF),
            V((HEADS, TOK, TOK), F32),
            V((TOK, HD), F32),
            V((TOK, HD), BF),
            V((TOK, HD), BF),
            V((TOK, HD), BF),
            V((TOK, HD), BF),
            V((TOK, D), BF),
            V((TOK, D), BF),
            V((TOK, TOK), F32),
            dma((5,)), dma((4,)),
            dma((2, 2, 4)), dma((2, 2, 4)),
            dma((8, 2)), dma((8, 2)),
            dma((8, 2, 2)), dma((8, 2, 2)),
            dma((8, 2, 2)), dma((8, 2, 2)),
            dma((8, 2)), dma((8, 2)),
            dma((8, 2)), dma((8, 2)),
            dma((2, 2, 4)), dma((2, 2, 4)),
            dma((8,)), dma((8,)),
            dma((3,)), dma((3,)),
        ],
        compiler_params=pltpu.CompilerParams(
            collective_id=0, has_side_effects=True, vmem_limit_bytes=60 * 2**20
        ),
        cost_estimate=pl.CostEstimate(flops=10**10, bytes_accessed=2 * 10**7, transcendentals=10**6),
    )(segment_ids, weight_codes, weight_exponents, queries, keys, values, out_grad, residual_in)
    return layer_out, query_grad, key_grad, value_grad, weight_grad


def solution(mesh):
    tokens = P(("outer", "inner"), None)
    in_specs = (tokens, tokens, tokens, tokens, tokens, P("inner", None), P("inner", None), tokens)
    out_specs = (tokens, tokens, tokens, tokens, P("inner", "outer"))
    return jax.shard_map(block_step, mesh=mesh, in_specs=in_specs, out_specs=out_specs, check_vma=False)
```

time: 632 us -> 111 us (0.18)
  waiting for transfers between devices: 440 us -> 0 us
  matrix products: 110 us -> 0 us
  Pallas kernels: 0 us -> 102 us
  local copies, waits for them, and re-layouts: 43.2 us -> 8.26 us
  other arithmetic: 17.8 us -> 0 us
  between operations: 14.6 us -> 0.65 us
    unnamed x4 -> x0, waiting for transfers between devices: 249 us -> none
    all_gather x1 -> x0, waiting for transfers between devices: 125 us -> none  [body(): lax.all_gather(weight_part, 'inner', axis=0, tiled=True)]
    dot_general x94 -> x0, matrix products: 110 us -> none  [the longest x26 28.4 us: head_probs(): lax.dot_general(query, key_rows, (((1,), (1,)), ((), ())), preferred_elem...]
    pallas_call x0 -> x1, Pallas kernels: none -> 102 us  [block_step(): pl.pallas_call(body_kernel, out_shape=(jax.ShapeDtypeStruct((TOK, D), BF)...]
    reduce_scatter x1 -> x0, waiting for transfers between devices: 66.1 us -> none  [body(): lax.psum_scatter(row_share, 'outer', scatter_dimension=1, tiled=True)]
    dynamic_update_slice x65 -> x0, local copies, waits for them, and re-layouts: 21.1 us -> none  [pack_forward(): lax.map(one_head, (heads_first(queries), heads_first(keys), heads_first(v...]
    reduce_sum x39 -> x0, other arithmetic: 14.4 us -> none  [the longest x13 12.5 us: one_head(): jnp.sum(output_grad.astype(jnp.float32) * output.astype(jnp.float32), axi...]
    unnamed x28 -> x14, local copies, waits for them, and re-layouts: 19.1 us -> 8.26 us
  transfers between devices with their start and end apart: 3 -> 0, of which waited for: 3 -> 0; matrix products, arithmetic and copies ran while one was open for 1% -> 0% of each run, Pallas kernels for 0% -> 0%
where the time goes in v1:
time: 111 us
  Pallas kernels  102 us (92%)
  local copies, waits for them, and re-layouts  8.26 us (7%)
    pallas_call x1, Pallas kernels, block_step(): pl.pallas_call(body_kernel, out_shape=(jax.ShapeDtypeStruct((TOK, D), BF)...  102 us
    unnamed x14, local copies, waits for them, and re-layouts  8.26 us

profile of v1, /device:TPU:1, one launch (start us, length us, event | category | flops | bytes accessed | tf_op | source)
XLA Modules:
  0.0 110.5 jit_solution(9943257236266491568)
XLA Ops:
  0.6 1.6 %copy.13.exps_ref = s32[200,52]{1,0:T(8,128)} copy(s32[200,52]{0,1:T(8,128)} %param.14) | data formatting | bytes 83200 | tf_op args[6]
  2.2 101.6 %shard_map.119 = (bf16[256,3200]{1,0:T(8,128)(2,1)}, bf16[256,1664]{1,0:T(8,128)(2,1)}, bf16[256,1664]{1,0:T(8,128)(2,1)}, bf16[256,1664]{1,0:T(8,128)(2,1)}, f32[200,104]{1,0:T(8,128)}) custom-call(s32[1,256]{1,0:T(1,128)} %seg_ref.1, bf16[200,1664]{1,0:T(8,128)(2,1)} %codes_ref.1, s32[200,52]{1,0:T(8,128)} %copy.13.exps_ref, bf16[256,1664]{1,0:T(8,128)(2,1)} %q_hbm.1, ...), custom_call_target="tpu_custom_call" | custom-call | flops 10000000000 | bytes 20000000 | tf_op jit(solution)/shard_map/pallas_call | solution.py:584
  103.8 0.0 copy-start.2
  103.8 2.8 %copy.19 = bf16[256,3200]{1,0:T(8,128)(2,1)} copy(bf16[256,3200]{1,0:T(8,128)(2,1)} %get-tuple-element.10) | data formatting | bytes 3276800
  106.6 0.0 copy-done.2
  106.6 0.0 copy-start.1
  106.6 0.0 copy-start
  106.6 0.9 copy.20
  107.5 0.6 copy-done.1
  108.1 0.0 copy-start.3
  108.1 0.9 copy.21
  109.0 0.0 copy-done
  109.0 0.9 copy.22
  109.9 0.0 copy-done.3
  109.9 0.6 copy.23
Async XLA Ops:
  103.8 2.8 %copy-start.2 = (bf16[256,1664]{1,0:T(8,128)(2,1)S(1)}, bf16[256,1664]{1,0:T(8,128)(2,1)}, u32[]{:S(2)}) copy-start(bf16[256,1664]{1,0:T(8,128)(2,1)} %get-tuple-element.11) | copy-start | bytes 2555908
  106.6 1.5 %copy-start.1 = (bf16[256,1664]{1,0:T(8,128)(2,1)S(1)}, bf16[256,1664]{1,0:T(8,128)(2,1)}, u32[]{:S(2)}) copy-start(bf16[256,1664]{1,0:T(8,128)(2,1)} %get-tuple-element.12) | copy-start | bytes 2555908
  106.6 2.4 %copy-start = (bf16[256,1664]{1,0:T(8,128)(2,1)S(1)}, bf16[256,1664]{1,0:T(8,128)(2,1)}, u32[]{:S(2)}) copy-start(bf16[256,1664]{1,0:T(8,128)(2,1)} %get-tuple-element.13) | copy-start | bytes 2555908
  108.1 1.8 %copy-start.3 = (f32[200,104]{1,0:T(8,128)S(1)}, f32[200,104]{1,0:T(8,128)}, u32[]{:S(2)}) copy-start(f32[200,104]{1,0:T(8,128)} %get-tuple-element.14) | copy-start | bytes 249604

commit v2 on v1

--- a/solution.py
+++ b/solution.py
@@ -25,6 +25,23 @@
 SHARE = 512
 TOP = (4, 3)
 
+PLAN = (
+    ("load", 4), ("load", 6), ("og", 0, 4), ("load", 5), ("load", 3), ("fwd", 0, 2), ("og", 4, 8), ("fwd", 2, 4),
+    ("zero",), ("fwd", 4, 6), ("ogs",), ("Z", 1), ("Z", 2), ("fwd", 6, 8), ("fwd", 8, 10), ("Z", 3), ("YA", 1),
+    ("fwd", 10, 12), ("load", 7), ("fwd", 12, 13), ("ord",), ("X", 0), ("Z", 4), ("ats",), ("X", 1), ("shares",),
+    ("YA", 2), ("part", 0, 1), ("YA", 3), ("part", 1, 2), ("X", 2), ("YA", 4), ("Z", 5), ("X", 3), ("ay", 0, 1),
+    ("Z", 6), ("S", 0), ("part", 2, 3), ("ax", 0, 1), ("E", 1, 0), ("gz", 4), ("S", 1), ("YB", 0), ("YA", 5),
+    ("YB", 1), ("X", 4), ("G", 1, 0), ("ay", 1, 2), ("S", 2), ("part", 3, 4), ("YB", 2), ("G", 1, 1), ("E", 1, 1),
+    ("ay", 2, 3), ("YB", 3), ("ax", 1, 2), ("part", 4, 5), ("ax", 2, 3), ("Z", 7), ("YA", 6), ("S", 3), ("YB", 4),
+    ("gz", 3), ("S", 4), ("X", 5), ("part", 5, 6), ("ay", 3, 4), ("G", 0, 1), ("E", 0, 1), ("ax", 3, 4), ("S", 5),
+    ("G", 0, 2), ("E", 1, 2), ("X", 6), ("part", 6, 7), ("ay", 4, 5), ("S", 6), ("YB", 5), ("E", 0, 2), ("E", 1, 3),
+    ("YB", 6), ("ax", 4, 5), ("gz", 2), ("E", 0, 3), ("ay", 5, 6), ("X", 7), ("ay", 6, 7), ("part", 7, 8),
+    ("ax", 5, 6), ("YA", 7), ("YB", 7), ("G", 0, 3), ("G", 0, 0), ("S", 7), ("E", 0, 4), ("E", 1, 4), ("ax", 6, 7),
+    ("gz", 1), ("ay", 7, 8), ("G", 1, 4), ("E", 0, 0), ("round",), ("bwd", 0, 2), ("ax", 7, 8), ("bwd", 2, 4),
+    ("bwd", 4, 6), ("G", 1, 3), ("gz", 0), ("last",), ("bwd", 6, 8), ("bwd", 8, 10), ("bwd", 10, 12), ("G", 1, 2),
+    ("G", 0, 4), ("fin",), ("bwd", 12, 13),
+)
+
 
 def chain(way, half):
     return TOP[half] if way == 0 else TOP[1 - half]
@@ -39,10 +56,10 @@
 
 
 def body_kernel(
-    seg_ref, codes_ref, exps_ref, q_hbm, k_hbm, v_hbm, og_hbm, res_hbm,
-    lo_hbm, dq_hbm, dk_hbm, dv_hbm, wg_ref,
-    W, PG, YR, XR, ZR, LB, FR, SR, SS, OGR, OGS, ATR, ATT, PST, AGF, AGB, Q, K, V, OG, LO, BIAS,
-    in_sem, out_sem, zs, zr, xs, xr, ys, yr, ss, sr, gys, gyr, gxs, gxr, gzs, gzr, fs, fr, cs, cr,
+    seg_hbm, codes_hbm, exps_hbm, q_hbm, k_hbm, v_hbm, og_hbm, res_hbm,
+    LO, Q, K, V, wg_ref,
+    W, PG, YR, XR, ZR, LB, FR, SR, SS, OGR, OGS, ATR, ATT, PST, AGF, AGB, OG, BIAS, CODES, EXPS, SEG,
+    in_sem, zs, zr, xs, xr, ys, yr, ss, sr, gys, gyr, gxs, gxr, gzs, gzr, fs, fr, cs, cr,
 ):
     o = lax.axis_index("outer")
     i = lax.axis_index("inner")
@@ -81,21 +98,23 @@
             src_ref=src, dst_ref=dst, send_sem=ssem, recv_sem=rsem, device_id=dev, device_id_type=MESH
         )
 
-    loads = [
-        pltpu.make_async_copy(src, dst, in_sem.at[n])
-        for n, (src, dst) in enumerate(
-            ((og_hbm, OG), (q_hbm, Q), (k_hbm, K), (v_hbm, V), (res_hbm, LO))
-        )
-    ]
     barrier = pltpu.get_barrier_semaphore()
     greet = [along_z(1), along_z(-1), along_x(1), along_x(-1), along_y(1), along_y(-1), sibling]
     greet += [owner_device(2, 0), owner_device(0, 1), owner_device(1, 1), owner_device(2, 1), owner_device(3, 1)]
     for dev in greet:
         pl.semaphore_signal(barrier, inc=1, device_id=dev, device_id_type=MESH)
+    loads = [
+        pltpu.make_async_copy(src, dst, in_sem.at[n])
+        for n, (src, dst) in enumerate(
+            ((codes_hbm, CODES), (exps_hbm, EXPS), (seg_hbm, SEG), (q_hbm, Q), (k_hbm, K), (v_hbm, V), (og_hbm, OG), (res_hbm, LO))
+        )
+    ]
     for load in loads:
         load.start()
 
-    exps = exps_ref[...]
+    for n in range(3):
+        loads[n].wait()
+    exps = EXPS[...]
     scale = jnp.zeros(exps.shape, F32)
     for octave in range(-16, 1):
         scale = scale + jnp.where(exps == octave, 2.0**octave, 0.0)
@@ -103,8 +122,8 @@
         lax.broadcasted_iota(jnp.int32, (HD // BLOCK, HD), 1) // BLOCK
         == lax.broadcasted_iota(jnp.int32, (HD // BLOCK, HD), 0)
     ).astype(BF)
-    wide = jnp.dot(scale.astype(BF), spread, preferred_element_type=F32)
-    block = codes_ref[...].astype(F32) * wide
+    wide = dot(scale.astype(BF), spread, 0, 0)
+    block = CODES[...].astype(F32) * wide
     block = jnp.concatenate([block, jnp.zeros((RP - RB, HD), F32)], axis=0)
     W[xl * 8 + z] = block.astype(BF)
 
@@ -180,17 +199,13 @@
                 x_copy(e, half).wait_recv()
                 spread_out(e, half)
 
-    def serve_y(n):
-        def go():
+    def serve_y(n, role):
+        @pl.when(role)
+        def _():
             for e, half in chunks[n]:
                 for way in (0, 1):
                     y_arrival(e, half, way).wait_recv()
                 s_copy(e, half, 1).start()
-
-        if n == 0:
-            pl.when(is_b)(go)
-        else:
-            go()
 
     @pl.when(is_a)
     def _():
@@ -199,7 +214,7 @@
                 z_copy(way, half, 1).start()
             x_copy(0, half).start()
 
-    seg = jnp.broadcast_to(seg_ref[...].astype(F32), (TOK, TOK))
+    seg = jnp.broadcast_to(SEG[...].astype(F32), (TOK, TOK))
     BIAS[...] = jnp.where(seg == seg.T, 0.0, -1e30)
     factor = 1.0 / math.sqrt(T)
 
@@ -399,15 +414,16 @@
         share.start()
         wg_ref[...] = jnp.where(c == 0, main, second)[0:RB, 0:104]
 
-    def grad_in(kz, carry):
+    def grad_in(who, e):
+        kz = zz(e)
+        lhs = OGR[kz, 0:TOK, 0:RP] if who == 0 else OGS[kz, :, 0:RP]
+        b = mine(e) if who == 0 else theirs(e)
         for start, size in ((0, 512), (512, 640), (1152, 512)):
             cols = pl.ds(start, size)
-            AGF[:, cols] += dot(OGR[kz, 0:TOK, 0:RP], W[c * 8 + kz, :, cols], 1, 0) + dot(
-                OGS[kz, :, 0:RP], W[(1 - c) * 8 + kz, :, cols], 1, 0
-            )
-        return carry
-
-    def project(b, carry):
+            AGF[:, cols] += dot(lhs, W[b, :, cols], 1, 0)
+
+    def project(who, e):
+        b = mine(e) if who == 0 else theirs(e)
         prod = dot(ATT[...], W[b], 1, 1)
         lane = lanes(TOK)
         first = (RB * b) // T
@@ -425,7 +441,6 @@
         put(0, lane >= shift, one)
         put(1, lane - shift < RB - T, jnp.where(lane < shift, one, two))
         put(2, lane < shift - (2 * T - RB), two)
-        return carry
 
     def backward(h, carry):
         cols = head_columns(h)
@@ -442,87 +457,63 @@
     def loop(low, high, what):
         lax.fori_loop(low, high, what, 0)
 
-    for load in loads:
-        load.wait()
-    loop(0, 8, og_blocks)
-    og_share.start()
-    loop(0, 4, forward)
-    serve_z(1)
-    serve_x(0)
-    loop(4, 8, forward)
-    serve_z(2)
-    serve_x(1)
-    loop(8, 13, forward)
-    loop(0, 4, order_columns)
-    at_share.start()
-    serve_z(3)
-    serve_x(2)
-    serve_y(0)
-    serve_y(1)
-    og_share.wait()
-    at_share.wait()
-    loop(0, 2, partial_product)
-    serve_z(4)
-    serve_x(3)
-    serve_y(2)
-    loop(2, 4, partial_product)
-    serve_z(5)
-    serve_x(4)
-    serve_y(3)
-    loop(4, 6, partial_product)
-    serve_z(6)
-    serve_x(5)
-    serve_y(4)
-    loop(6, 8, partial_product)
-    serve_z(7)
-    serve_x(6)
-    serve_y(5)
-    AGF[...] = jnp.zeros((TOK, HD), F32)
-    loop(0, 2, add_y)
-    serve_x(7)
-    serve_y(6)
-    loop(2, 4, add_y)
-    serve_y(7)
-
-    for n in range(8):
+    def blocks(what, who, group):
+        low = group % 4
+        if low == 0:
+            what(who, group)
+        else:
+            def go(n, carry):
+                what(who, low + n * (8 - 2 * low))
+                return carry
+
+            loop(0, 2, go)
+
+    def serve_s(n):
         for e, half in chunks[n]:
-            for kind in (0, 1):
-                if e == 0:
-                    @pl.when(is_a)
-                    def _():
-                        s_copy(e, half, kind, theirs).wait_recv()
-                else:
+            def go(e=e, half=half):
+                for kind in (0, 1):
                     s_copy(e, half, kind, theirs).wait_recv()
 
-    loop(0, 1, add_x)
-    serve_gz(4)
-    loop(0, 4, grad_in)
-    loop(4, 5, add_y)
-    loop(1, 3, add_x)
-    serve_gz(3)
-    loop(4, 8, grad_in)
-    AGB[...] = AGF[...].astype(BF)
-    loop(5, 6, add_y)
-    loop(0, 4, backward)
-    loop(6, 8, add_y)
-    loop(3, 5, add_x)
-    serve_gz(2)
-    loop(4, 8, backward)
-    loop(5, 7, add_x)
-    serve_gz(1)
-    loop(8, 13, backward)
-    outs = [
-        pltpu.make_async_copy(src, dst, out_sem.at[n])
-        for n, (src, dst) in enumerate(((Q, dq_hbm), (K, dk_hbm), (V, dv_hbm), (LO, lo_hbm)))
-    ]
-    for n in range(3):
-        outs[n].start()
-    loop(7, 8, add_x)
-    serve_gz(0)
-    pl.when(is_a)(send_last)
-    loop(0, 16, project)
-    outs[3].start()
-    pl.when(is_a)(finish)
+            if e == 0:
+                pl.when(is_a)(go)
+            else:
+                go()
+
+    def zero_grad():
+        AGF[...] = jnp.zeros((TOK, HD), F32)
+
+    def round_grad():
+        AGB[...] = AGF[...].astype(BF)
+
+    def shares():
+        og_share.wait()
+        at_share.wait()
+
+    does = {
+        "load": lambda n: loads[n].wait(),
+        "og": lambda a, b: loop(a, b, og_blocks),
+        "ogs": og_share.start,
+        "fwd": lambda a, b: loop(a, b, forward),
+        "ord": lambda: loop(0, 4, order_columns),
+        "ats": at_share.start,
+        "shares": shares,
+        "Z": serve_z, "X": serve_x, "S": serve_s,
+        "YA": lambda n: serve_y(n, is_a),
+        "YB": lambda n: serve_y(n, is_b),
+        "part": lambda a, b: loop(a, b, partial_product),
+        "ay": lambda a, b: loop(a, b, add_y),
+        "ax": lambda a, b: loop(a, b, add_x),
+        "gz": serve_gz,
+        "zero": zero_grad,
+        "E": lambda who, group: blocks(grad_in, who, group),
+        "G": lambda who, group: blocks(project, who, group),
+        "round": round_grad,
+        "bwd": lambda a, b: loop(a, b, backward),
+        "last": lambda: pl.when(is_a)(send_last),
+        "fin": lambda: pl.when(is_a)(finish),
+    }
+    for name, *args in PLAN:
+        does[name](*args)
 
     @pl.when(is_b)
     def _():
@@ -572,8 +563,14 @@
             f_copy(dy, dx).wait_send()
         share.wait_send()
 
-    for out in outs:
-        out.wait()
+
+def store_kernel(*refs):
+    sems = refs[-1]
+    copies = [pltpu.make_async_copy(refs[n], refs[5 + n], sems.at[n]) for n in range(5)]
+    for copy in copies:
+        copy.start()
+    for copy in copies:
+        copy.wait()
 
 
 def block_step(residual_in, queries, keys, values, segment_ids, weight_codes, weight_exponents, out_grad):
@@ -581,17 +578,14 @@
     hbm = pl.BlockSpec(memory_space=pl.ANY)
     dma = pltpu.SemaphoreType.DMA
     V = pltpu.VMEM
-    layer_out, query_grad, key_grad, value_grad, weight_grad = pl.pallas_call(
+    shapes = (((TOK, D), BF), ((TOK, HD), BF), ((TOK, HD), BF), ((TOK, HD), BF), ((RB, 104), F32))
+    args = (segment_ids, weight_codes, weight_exponents.T, queries, keys, values, out_grad, residual_in)
+    args = [pltpu.with_memory_space_constraint(arg, pltpu.HBM) for arg in args]
+    outs = pl.pallas_call(
         body_kernel,
-        out_shape=(
-            jax.ShapeDtypeStruct((TOK, D), BF),
-            jax.ShapeDtypeStruct((TOK, HD), BF),
-            jax.ShapeDtypeStruct((TOK, HD), BF),
-            jax.ShapeDtypeStruct((TOK, HD), BF),
-            jax.ShapeDtypeStruct((RB, 104), F32),
-        ),
-        in_specs=[vmem] * 3 + [hbm] * 5,
-        out_specs=(hbm, hbm, hbm, hbm, vmem),
+        out_shape=tuple(V(*shape) for shape in shapes),
+        in_specs=[pl.BlockSpec(memory_space=pltpu.HBM)] * 8,
+        out_specs=(vmem,) * 5,
         scratch_shapes=[
             V((16, RP, HD), BF),
             V((8, RP, HD), BF),
@@ -609,13 +603,12 @@
             V((HEADS, TOK, TOK), F32),
             V((TOK, HD), F32),
             V((TOK, HD), BF),
-            V((TOK, HD), BF),
-            V((TOK, HD), BF),
-            V((TOK, HD), BF),
-            V((TOK, D), BF),
             V((TOK, D), BF),
             V((TOK, TOK), F32),
-            dma((5,)), dma((4,)),
+            V((RB, HD), BF),
+            V((HD // BLOCK, RB), jnp.int32),
+            V((1, TOK), jnp.int32),
+            dma((8,)),
             dma((2, 2, 4)), dma((2, 2, 4)),
             dma((8, 2)), dma((8, 2)),
             dma((8, 2, 2)), dma((8, 2, 2)),
@@ -627,11 +620,19 @@
             dma((3,)), dma((3,)),
         ],
         compiler_params=pltpu.CompilerParams(
-            collective_id=0, has_side_effects=True, vmem_limit_bytes=60 * 2**20
+            collective_id=0, has_side_effects=True, vmem_limit_bytes=48 * 2**20
         ),
         cost_estimate=pl.CostEstimate(flops=10**10, bytes_accessed=2 * 10**7, transcendentals=10**6),
-    )(segment_ids, weight_codes, weight_exponents, queries, keys, values, out_grad, residual_in)
-    return layer_out, query_grad, key_grad, value_grad, weight_grad
+    )(*args)
+    outs = [pltpu.with_memory_space_constraint(out, pltpu.VMEM) for out in outs]
+    return pl.pallas_call(
+        store_kernel,
+        out_shape=tuple(jax.ShapeDtypeStruct(*shape) for shape in shapes),
+        in_specs=[hbm] * 5,
+        out_specs=(hbm,) * 5,
+        scratch_shapes=[dma((5,))],
+        compiler_params=pltpu.CompilerParams(vmem_limit_bytes=2**20),
+    )(*outs)
 
 
 def solution(mesh):

time: 111 us -> 84.9 us (0.76)
  Pallas kernels: 102 us -> 84.1 us
  local copies, waits for them, and re-layouts: 8.26 us -> 0 us
    pallas_call x1 -> x2, Pallas kernels: 102 us -> 84.1 us  [the longest x1 82 us: block_step(): pl.pallas_call(body_kernel, out_shape=tuple((V(*shape) for shape in shape...]
    unnamed x14 -> x0, local copies, waits for them, and re-layouts: 8.26 us -> none
where the time goes in v2:
time: 84.9 us
  Pallas kernels  84.1 us (99%)
    pallas_call x1, Pallas kernels, block_step(): pl.pallas_call(body_kernel, out_shape=tuple((V(*shape) for shape in shape...  82 us
    pallas_call x1, Pallas kernels, block_step(): pl.pallas_call(store_kernel, out_shape=tuple((jax.ShapeDtypeStruct(*shape...  2.07 us

profile of v2, /device:TPU:1, one launch (start us, length us, event | category | flops | bytes accessed | tf_op | source)
XLA Modules:
  0.0 84.9 jit_solution(3062095959702426013)
XLA Ops:
  0.6 82.0 %shard_map.119 = (bf16[256,3200]{1,0:T(8,128)(2,1)S(1)}, bf16[256,1664]{1,0:T(8,128)(2,1)S(1)}, bf16[256,1664]{1,0:T(8,128)(2,1)S(1)}, bf16[256,1664]{1,0:T(8,128)(2,1)S(1)}, f32[200,104]{1,0:T(8,128)S(1)}) custom-call(s32[1,256]{1,0:T(1,128)} %seg_hbm.1, bf16[200,1664]{1,0:T(8,128)(2,1)} %codes_hbm.1, s32[52,200]{1,0:T(8,128)} %bitcast.1, ...), custom_call_target="tpu_custom_call" | custom-call | flops 10000000000 | bytes 20000000 | tf_op jit(solution)/shard_map/pallas_call | solution.py:584
  82.6 2.1 %shard_map.120 = (bf16[256,3200]{1,0:T(8,128)(2,1)}, bf16[256,1664]{1,0:T(8,128)(2,1)}, bf16[256,1664]{1,0:T(8,128)(2,1)}, bf16[256,1664]{1,0:T(8,128)(2,1)}, f32[200,104]{1,0:T(8,128)}) custom-call(bf16[256,3200]{1,0:T(8,128)(2,1)S(1)} %get-tuple-element.10.refs_0_, bf16[256,1664]{1,0:T(8,128)(2,1)S(1)} %get-tuple-element.11.refs_1_, ...), custom_call_target="tpu_custom_call" | custom-call | tf_op jit(solution)/shard_map/pallas_call | solution.py:628

commit v3 on v2

--- a/solution.py
+++ b/solution.py
@@ -25,21 +25,23 @@
 SHARE = 512
 TOP = (4, 3)
 
+GROUPS = ((0,), (7, 1), (6, 2), (5, 3), (4,))
+
 PLAN = (
-    ("load", 4), ("load", 6), ("og", 0, 4), ("load", 5), ("load", 3), ("fwd", 0, 2), ("og", 4, 8), ("fwd", 2, 4),
-    ("zero",), ("fwd", 4, 6), ("ogs",), ("Z", 1), ("Z", 2), ("fwd", 6, 8), ("fwd", 8, 10), ("Z", 3), ("YA", 1),
-    ("fwd", 10, 12), ("load", 7), ("fwd", 12, 13), ("ord",), ("X", 0), ("Z", 4), ("ats",), ("X", 1), ("shares",),
-    ("YA", 2), ("part", 0, 1), ("YA", 3), ("part", 1, 2), ("X", 2), ("YA", 4), ("Z", 5), ("X", 3), ("ay", 0, 1),
-    ("Z", 6), ("S", 0), ("part", 2, 3), ("ax", 0, 1), ("E", 1, 0), ("gz", 4), ("S", 1), ("YB", 0), ("YA", 5),
-    ("YB", 1), ("X", 4), ("G", 1, 0), ("ay", 1, 2), ("S", 2), ("part", 3, 4), ("YB", 2), ("G", 1, 1), ("E", 1, 1),
-    ("ay", 2, 3), ("YB", 3), ("ax", 1, 2), ("part", 4, 5), ("ax", 2, 3), ("Z", 7), ("YA", 6), ("S", 3), ("YB", 4),
-    ("gz", 3), ("S", 4), ("X", 5), ("part", 5, 6), ("ay", 3, 4), ("G", 0, 1), ("E", 0, 1), ("ax", 3, 4), ("S", 5),
-    ("G", 0, 2), ("E", 1, 2), ("X", 6), ("part", 6, 7), ("ay", 4, 5), ("S", 6), ("YB", 5), ("E", 0, 2), ("E", 1, 3),
-    ("YB", 6), ("ax", 4, 5), ("gz", 2), ("E", 0, 3), ("ay", 5, 6), ("X", 7), ("ay", 6, 7), ("part", 7, 8),
-    ("ax", 5, 6), ("YA", 7), ("YB", 7), ("G", 0, 3), ("G", 0, 0), ("S", 7), ("E", 0, 4), ("E", 1, 4), ("ax", 6, 7),
-    ("gz", 1), ("ay", 7, 8), ("G", 1, 4), ("E", 0, 0), ("round",), ("bwd", 0, 2), ("ax", 7, 8), ("bwd", 2, 4),
-    ("bwd", 4, 6), ("G", 1, 3), ("gz", 0), ("last",), ("bwd", 6, 8), ("bwd", 8, 10), ("bwd", 10, 12), ("G", 1, 2),
-    ("G", 0, 4), ("fin",), ("bwd", 12, 13),
+    ("load", 6), ("load", 3), ("og", 0, 4), ("load", 4), ("load", 5), ("fwd", 0, 2), ("og", 4, 8), ("fwd", 2, 4),
+    ("fwd", 4, 6), ("ogs",), ("Z", 1), ("fwd", 6, 8), ("fwd", 8, 10), ("fwd", 10, 12), ("Z", 2), ("fwd", 12, 13),
+    ("Z", 3), ("ord",), ("ats",), ("X", 0), ("X", 1), ("shares",), ("part", 0, 1), ("Z", 4), ("zero",),
+    ("part", 1, 2), ("part", 2, 3), ("Z", 5), ("ay", 0, 1), ("Z", 6), ("YA", 1), ("part", 3, 4), ("X", 2), ("YA", 2),
+    ("load", 7), ("ax", 0, 1), ("YA", 3), ("part", 4, 5), ("YB", 0), ("gz", 4), ("X", 3), ("ay", 1, 2), ("ay", 2, 3),
+    ("X", 4), ("S", 0), ("ax", 1, 2), ("ay", 3, 4), ("YB", 1), ("part", 5, 6), ("ay", 4, 5), ("YA", 4),
+    ("part", 6, 7), ("ax", 2, 3), ("YB", 2), ("X", 5), ("gz", 3), ("E", 1, 0), ("X", 6), ("E", 0, 1), ("YA", 5),
+    ("G", 1, 0), ("YB", 3), ("ay", 5, 6), ("part", 7, 8), ("S", 1), ("ax", 3, 4), ("E", 0, 0), ("Z", 7), ("YB", 4),
+    ("ax", 4, 5), ("gz", 2), ("G", 0, 2), ("ay", 6, 7), ("X", 7), ("S", 2), ("E", 0, 2), ("ax", 5, 6), ("YB", 5),
+    ("YB", 6), ("YA", 6), ("G", 0, 3), ("S", 3), ("YA", 7), ("S", 4), ("ay", 7, 8), ("ax", 6, 7), ("YB", 7), ("S", 5),
+    ("S", 6), ("gz", 1), ("G", 0, 4), ("S", 7), ("E", 1, 3), ("G", 1, 1), ("E", 1, 4), ("G", 0, 0), ("E", 1, 1),
+    ("E", 0, 3), ("E", 0, 4), ("G", 0, 1), ("E", 1, 2), ("ax", 7, 8), ("gz", 0), ("last",), ("G", 1, 2), ("G", 1, 4),
+    ("round",), ("bwd", 0, 2), ("bwd", 2, 4), ("G", 1, 3), ("bwd", 4, 6), ("bwd", 6, 8), ("bwd", 8, 10),
+    ("bwd", 10, 12), ("fin",), ("bwd", 12, 13),
 )
 
 
@@ -98,22 +100,24 @@
             src_ref=src, dst_ref=dst, send_sem=ssem, recv_sem=rsem, device_id=dev, device_id_type=MESH
         )
 
-    barrier = pltpu.get_barrier_semaphore()
-    greet = [along_z(1), along_z(-1), along_x(1), along_x(-1), along_y(1), along_y(-1), sibling]
-    greet += [owner_device(2, 0), owner_device(0, 1), owner_device(1, 1), owner_device(2, 1), owner_device(3, 1)]
-    for dev in greet:
-        pl.semaphore_signal(barrier, inc=1, device_id=dev, device_id_type=MESH)
     loads = [
         pltpu.make_async_copy(src, dst, in_sem.at[n])
         for n, (src, dst) in enumerate(
             ((codes_hbm, CODES), (exps_hbm, EXPS), (seg_hbm, SEG), (q_hbm, Q), (k_hbm, K), (v_hbm, V), (og_hbm, OG), (res_hbm, LO))
         )
     ]
-    for load in loads:
+    for load in loads[:3]:
         load.start()
-
-    for n in range(3):
-        loads[n].wait()
+    barrier = pltpu.get_barrier_semaphore()
+    greet = [along_z(1), along_z(-1), along_x(1), along_x(-1), along_y(1), along_y(-1), sibling]
+    greet += [owner_device(2, 0), owner_device(0, 1), owner_device(1, 1), owner_device(2, 1), owner_device(3, 1)]
+    for dev in greet:
+        pl.semaphore_signal(barrier, inc=1, device_id=dev, device_id_type=MESH)
+
+    for load in loads[3:]:
+        load.start()
+    for load in loads[:3]:
+        load.wait()
     exps = EXPS[...]
     scale = jnp.zeros(exps.shape, F32)
     for octave in range(-16, 1):
@@ -189,14 +193,20 @@
                 z_arrival(way, half, step).wait_recv()
                 if step < chain(way, half):
                     z_copy(way, half, step + 1).start()
-                x_copy(e, half).start()
+                if e != 4:
+                    x_copy(e, half).start()
                 spread_out(e, half)
 
     def serve_x(n):
         @pl.when(is_b)
         def _():
             for e, half in chunks[n]:
-                x_copy(e, half).wait_recv()
+                if e == 4:
+                    z_arrival(half, half, 4).wait_recv()
+                else:
+                    x_copy(e, half).wait_recv()
+                if (e, half) in ((5, 0), (3, 1)):
+                    z_copy(half, half, 4).start()
                 spread_out(e, half)
 
     def serve_y(n, role):
@@ -219,16 +229,21 @@
     factor = 1.0 / math.sqrt(T)
 
     def head_columns(h):
-        return pl.ds(pl.multiple_of(h * T, T), T)
-
-    def forward(h, carry):
-        cols = head_columns(h)
-        s = dot(Q[:, cols], K[:, cols], 1, 1) * factor + BIAS[...]
-        s = jnp.exp(s - jnp.max(s, axis=1, keepdims=True))
-        p = s * (1.0 / jnp.sum(s, axis=1, keepdims=True))
-        PST[h] = p
-        ATT[:, cols] = dot(p.astype(BF), V[:, cols], 1, 0).astype(BF)
-        return carry
+        return slice(h * T, (h + 1) * T)
+
+    def forward(low, high):
+        cols = [head_columns(h) for h in range(low, high)]
+        qs, ks, vs = [[ref[:, col] for col in cols] for ref in (Q, K, V)]
+        bias = BIAS[...]
+        scores = [dot(q, k, 1, 1) * factor + bias for q, k in zip(qs, ks)]
+        tops = [jnp.max(s, axis=1, keepdims=True) for s in scores]
+        scores = [jnp.exp(s - top) for s, top in zip(scores, tops)]
+        sums = [1.0 / jnp.sum(s, axis=1, keepdims=True) for s in scores]
+        probs = [s * inverse for s, inverse in zip(scores, sums)]
+        outs = [dot(p.astype(BF), v, 1, 0).astype(BF) for p, v in zip(probs, vs)]
+        for n, h in enumerate(range(low, high)):
+            PST[h] = probs[n]
+            ATT[:, cols[n]] = outs[n]
 
     def og_blocks(kz, carry):
         lane = lanes(TOK)
@@ -414,59 +429,61 @@
         share.start()
         wg_ref[...] = jnp.where(c == 0, main, second)[0:RB, 0:104]
 
-    def grad_in(who, e):
-        kz = zz(e)
-        lhs = OGR[kz, 0:TOK, 0:RP] if who == 0 else OGS[kz, :, 0:RP]
-        b = mine(e) if who == 0 else theirs(e)
+    def block(who, e):
+        return mine(e) if who == 0 else theirs(e)
+
+    def grad_in(who, group):
         for start, size in ((0, 512), (512, 640), (1152, 512)):
             cols = pl.ds(start, size)
-            AGF[:, cols] += dot(lhs, W[b, :, cols], 1, 0)
-
-    def project(who, e):
-        b = mine(e) if who == 0 else theirs(e)
-        prod = dot(ATT[...], W[b], 1, 1)
+            prods = [
+                dot(OGR[zz(e), 0:TOK, 0:RP] if who == 0 else OGS[zz(e), :, 0:RP], W[block(who, e), :, cols], 1, 0)
+                for e in group
+            ]
+            AGF[:, cols] += sum(prods[1:], prods[0])
+
+    def project(who, group):
+        att = ATT[...]
         lane = lanes(TOK)
-        first = (RB * b) // T
-        shift = (RB * b) % T
-        one = pltpu.roll(prod[:, 0:T], shift, 1)
-        tail = jnp.concatenate([prod[:, T:RP], jnp.zeros((TOK, 2 * T - RP), F32)], axis=1)
-        two = pltpu.roll(tail, shift, 1)
-
-        def put(n, mask, value):
-            cols = pl.ds(pl.multiple_of(jnp.minimum(first + n, D // T - 1) * T, T), T)
-            old = LO[:, cols]
-            new = (old.astype(F32) + value).astype(BF)
-            LO[:, cols] = jnp.where(mask, new, old)
-
-        put(0, lane >= shift, one)
-        put(1, lane - shift < RB - T, jnp.where(lane < shift, one, two))
-        put(2, lane < shift - (2 * T - RB), two)
-
-    def backward(h, carry):
-        cols = head_columns(h)
-        p = PST[h]
-        dout = AGB[:, cols]
-        q, k, v = Q[:, cols], K[:, cols], V[:, cols]
-        delta = jnp.sum(dout.astype(F32) * ATT[:, cols].astype(F32), axis=1, keepdims=True)
-        ds = (p * (dot(dout, v, 1, 1) - delta)).astype(BF)
-        V[:, cols] = dot(p.astype(BF), dout, 0, 0).astype(BF)
-        Q[:, cols] = (dot(ds, k, 1, 0) * factor).astype(BF)
-        K[:, cols] = (dot(ds, q, 0, 0) * factor).astype(BF)
-        return carry
+        done = []
+        for e in group:
+            prod = dot(att, W[block(who, e)], 1, 1)
+            shift = (RB * block(who, e)) % T
+            one = pltpu.roll(prod[:, 0:T], shift, 1)
+            tail = jnp.concatenate([prod[:, T:RP], jnp.zeros((TOK, 2 * T - RP), F32)], axis=1)
+            two = pltpu.roll(tail, shift, 1)
+            done.append((shift, one, two))
+        for e, (shift, one, two) in zip(group, done):
+            first = (RB * block(who, e)) // T
+
+            def put(n, mask, value):
+                cols = pl.ds(pl.multiple_of(jnp.minimum(first + n, D // T - 1) * T, T), T)
+                old = LO[:, cols]
+                new = (old.astype(F32) + value).astype(BF)
+                LO[:, cols] = jnp.where(mask, new, old)
+
+            put(0, lane >= shift, one)
+            put(1, lane - shift < RB - T, jnp.where(lane < shift, one, two))
+            put(2, lane < shift - (2 * T - RB), two)
+
+    def backward(low, high):
+        cols = [head_columns(h) for h in range(low, high)]
+        qs, ks, vs, douts, atts = [[ref[:, col] for col in cols] for ref in (Q, K, V, AGB, ATT)]
+        probs = [PST[h] for h in range(low, high)]
+        deltas = [
+            jnp.sum(dout.astype(F32) * att.astype(F32), axis=1, keepdims=True) for dout, att in zip(douts, atts)
+        ]
+        prob_grads = [dot(dout, v, 1, 1) for dout, v in zip(douts, vs)]
+        grads = [(p * (g - delta)).astype(BF) for p, g, delta in zip(probs, prob_grads, deltas)]
+        dvs = [dot(p.astype(BF), dout, 0, 0).astype(BF) for p, dout in zip(probs, douts)]
+        dqs = [(dot(g, k, 1, 0) * factor).astype(BF) for g, k in zip(grads, ks)]
+        dks = [(dot(g, q, 0, 0) * factor).astype(BF) for g, q in zip(grads, qs)]
+        for n, col in enumerate(cols):
+            Q[:, col] = dqs[n]
+            K[:, col] = dks[n]
+            V[:, col] = dvs[n]
 
     def loop(low, high, what):
         lax.fori_loop(low, high, what, 0)
-
-    def blocks(what, who, group):
-        low = group % 4
-        if low == 0:
-            what(who, group)
-        else:
-            def go(n, carry):
-                what(who, low + n * (8 - 2 * low))
-                return carry
-
-            loop(0, 2, go)
 
     def serve_s(n):
         for e, half in chunks[n]:
@@ -493,7 +510,7 @@
         "load": lambda n: loads[n].wait(),
         "og": lambda a, b: loop(a, b, og_blocks),
         "ogs": og_share.start,
-        "fwd": lambda a, b: loop(a, b, forward),
+        "fwd": forward,
         "ord": lambda: loop(0, 4, order_columns),
         "ats": at_share.start,
         "shares": shares,
@@ -505,10 +522,10 @@
         "ax": lambda a, b: loop(a, b, add_x),
         "gz": serve_gz,
         "zero": zero_grad,
-        "E": lambda who, group: blocks(grad_in, who, group),
-        "G": lambda who, group: blocks(project, who, group),
+        "E": lambda who, n: grad_in(who, GROUPS[n]),
+        "G": lambda who, n: project(who, GROUPS[n]),
         "round": round_grad,
-        "bwd": lambda a, b: loop(a, b, backward),
+        "bwd": backward,
         "last": lambda: pl.when(is_a)(send_last),
         "fin": lambda: pl.when(is_a)(finish),
     }
@@ -548,10 +565,12 @@
             return carry
 
         loop(0, 8, sent_x)
+        for half in (0, 1):
+            z_copy(half, half, 4).wait_send()
 
     @pl.when(is_a)
     def _():
-        for e in range(8):
+        for e in (0, 1, 2, 3, 5, 6, 7):
             for half in (0, 1):
                 x_copy(e, half).wait_send()
         for half in (0, 1):

time: 84.9 us -> 82.4 us (0.971)
  Pallas kernels: 84.1 us -> 81.5 us
    pallas_call x1, Pallas kernels: 82 us -> 79.4 us  [block_step(): pl.pallas_call(body_kernel, out_shape=tuple((V(*shape) for shape in shape...]
where the time goes in v3:
time: 82.4 us; the launch traced here: 82.3 us
  Pallas kernels  81.5 us (99%)
    pallas_call x1, Pallas kernels, block_step(): pl.pallas_call(body_kernel, out_shape=tuple((V(*shape) for shape in shape...  79.4 us
    pallas_call x1, Pallas kernels, block_step(): pl.pallas_call(store_kernel, out_shape=tuple((jax.ShapeDtypeStruct(*shape...  2.07 us

profile of v3, /device:TPU:1, one launch (start us, length us, event | category | flops | bytes accessed | tf_op | source)
XLA Modules:
  0.0 82.3 jit_solution(5744289161795894552)
XLA Ops:
  0.6 79.4 %shard_map.119 = (bf16[256,3200]{1,0:T(8,128)(2,1)S(1)}, bf16[256,1664]{1,0:T(8,128)(2,1)S(1)}, bf16[256,1664]{1,0:T(8,128)(2,1)S(1)}, bf16[256,1664]{1,0:T(8,128)(2,1)S(1)}, f32[200,104]{1,0:T(8,128)S(1)}) custom-call(s32[1,256]{1,0:T(1,128)} %seg_hbm.1, bf16[200,1664]{1,0:T(8,128)(2,1)} %codes_hbm.1, s32[52,200]{1,0:T(8,128)} %bitcast.1, ...), custom_call_target="tpu_custom_call" | custom-call | flops 10000000000 | bytes 20000000 | tf_op jit(solution)/shard_map/pallas_call | solution.py:603
  80.0 2.1 %shard_map.120 = (bf16[256,3200]{1,0:T(8,128)(2,1)}, bf16[256,1664]{1,0:T(8,128)(2,1)}, bf16[256,1664]{1,0:T(8,128)(2,1)}, bf16[256,1664]{1,0:T(8,128)(2,1)}, f32[200,104]{1,0:T(8,128)}) custom-call(bf16[256,3200]{1,0:T(8,128)(2,1)S(1)} %get-tuple-element.10.refs_0_, bf16[256,1664]{1,0:T(8,128)(2,1)S(1)} %get-tuple-element.11.refs_1_, ...), custom_call_target="tpu_custom_call" | custom-call | tf_op jit(solution)/shard_map/pallas_call | solution.py:647

commit v4 on v3

--- a/solution.py
+++ b/solution.py
@@ -23,25 +23,26 @@
 SPAN = ((0, 112), (112, 96))
 CARRY = 1152
 SHARE = 512
+SPARE_X = True
 TOP = (4, 3)
 
 GROUPS = ((0,), (7, 1), (6, 2), (5, 3), (4,))
 
 PLAN = (
-    ("load", 6), ("load", 3), ("og", 0, 4), ("load", 4), ("load", 5), ("fwd", 0, 2), ("og", 4, 8), ("fwd", 2, 4),
-    ("fwd", 4, 6), ("ogs",), ("Z", 1), ("fwd", 6, 8), ("fwd", 8, 10), ("fwd", 10, 12), ("Z", 2), ("fwd", 12, 13),
-    ("Z", 3), ("ord",), ("ats",), ("X", 0), ("X", 1), ("shares",), ("part", 0, 1), ("Z", 4), ("zero",),
-    ("part", 1, 2), ("part", 2, 3), ("Z", 5), ("ay", 0, 1), ("Z", 6), ("YA", 1), ("part", 3, 4), ("X", 2), ("YA", 2),
-    ("load", 7), ("ax", 0, 1), ("YA", 3), ("part", 4, 5), ("YB", 0), ("gz", 4), ("X", 3), ("ay", 1, 2), ("ay", 2, 3),
-    ("X", 4), ("S", 0), ("ax", 1, 2), ("ay", 3, 4), ("YB", 1), ("part", 5, 6), ("ay", 4, 5), ("YA", 4),
-    ("part", 6, 7), ("ax", 2, 3), ("YB", 2), ("X", 5), ("gz", 3), ("E", 1, 0), ("X", 6), ("E", 0, 1), ("YA", 5),
-    ("G", 1, 0), ("YB", 3), ("ay", 5, 6), ("part", 7, 8), ("S", 1), ("ax", 3, 4), ("E", 0, 0), ("Z", 7), ("YB", 4),
-    ("ax", 4, 5), ("gz", 2), ("G", 0, 2), ("ay", 6, 7), ("X", 7), ("S", 2), ("E", 0, 2), ("ax", 5, 6), ("YB", 5),
-    ("YB", 6), ("YA", 6), ("G", 0, 3), ("S", 3), ("YA", 7), ("S", 4), ("ay", 7, 8), ("ax", 6, 7), ("YB", 7), ("S", 5),
-    ("S", 6), ("gz", 1), ("G", 0, 4), ("S", 7), ("E", 1, 3), ("G", 1, 1), ("E", 1, 4), ("G", 0, 0), ("E", 1, 1),
-    ("E", 0, 3), ("E", 0, 4), ("G", 0, 1), ("E", 1, 2), ("ax", 7, 8), ("gz", 0), ("last",), ("G", 1, 2), ("G", 1, 4),
-    ("round",), ("bwd", 0, 2), ("bwd", 2, 4), ("G", 1, 3), ("bwd", 4, 6), ("bwd", 6, 8), ("bwd", 8, 10),
-    ("bwd", 10, 12), ("fin",), ("bwd", 12, 13),
+    ("load", 6), ("load", 5), ("og", 0, 4), ("load", 4), ("og", 4, 8), ("load", 3), ("fwd", 0, 2), ("ogs",),
+    ("fwd", 2, 4), ("fwd", 4, 6), ("fwd", 6, 8), ("fwd", 8, 10), ("fwd", 10, 12), ("Z", 1), ("fwd", 12, 13), ("ord",),
+    ("ats",), ("X", 0), ("shares",), ("load", 7), ("part", 0, 1), ("X", 1), ("X", 2), ("Z", 2), ("Z", 3), ("YB", 0),
+    ("YA", 1), ("YA", 2), ("ay", 0, 1), ("YA", 3), ("part", 1, 2), ("YB", 1), ("Z", 4), ("X", 3), ("zero",),
+    ("ax", 0, 1), ("part", 2, 3), ("Z", 5), ("part", 3, 4), ("YB", 2), ("S", 0), ("gz", 4), ("ay", 1, 2), ("E", 0, 0),
+    ("S", 1), ("S", 2), ("Z", 6), ("S", 3), ("ay", 2, 3), ("YB", 3), ("part", 4, 5), ("YA", 4), ("ax", 1, 2),
+    ("part", 5, 6), ("ax", 2, 3), ("X", 4), ("G", 1, 0), ("gz", 3), ("X", 5), ("ay", 3, 4), ("ax", 3, 4), ("S", 4),
+    ("Z", 7), ("part", 6, 7), ("YA", 5), ("ay", 4, 5), ("E", 1, 1), ("YA", 6), ("E", 0, 1), ("X", 6), ("ax", 4, 5),
+    ("G", 0, 1), ("YB", 4), ("ay", 5, 6), ("gz", 2), ("part", 7, 8), ("G", 1, 2), ("ax", 5, 6), ("ay", 6, 7),
+    ("S", 5), ("YB", 5), ("YB", 6), ("G", 0, 2), ("YA", 7), ("S", 6), ("ax", 6, 7), ("gz", 1), ("X", 7), ("ay", 7, 8),
+    ("S", 7), ("G", 0, 3), ("YB", 7), ("E", 0, 4), ("ax", 7, 8), ("E", 0, 3), ("E", 1, 3), ("G", 1, 1), ("gz0", 0),
+    ("last", 0), ("G", 0, 4), ("E", 1, 0), ("E", 1, 4), ("gz0", 1), ("last", 1), ("E", 0, 2), ("G", 1, 3),
+    ("E", 1, 2), ("round",), ("bwd", 0, 2), ("bwd", 2, 4), ("G", 1, 4), ("bwd", 4, 6), ("bwd", 6, 8), ("bwd", 8, 10),
+    ("G", 0, 0), ("fin",), ("bwd", 10, 12), ("bwd", 12, 13),
 )
 
 
@@ -157,7 +158,7 @@
 
     def x_copy(e, half):
         part = W.at[mine(e), rows(half), pl.ds(own_col, CARRY)]
-        turn = (half + min(e, 8 - e)) % 2
+        turn = (half + (e > 4)) % 2
         return remote(part, part, xs.at[e, half], xr.at[e, half], along_x(1 - 2 * turn))
 
     def y_copy(e, half, way):
@@ -321,15 +322,15 @@
         return carry
 
     def gx_copy(e, half):
-        turn = (half + jnp.minimum(e, 8 - e)) % 2
+        turn = (half + min(e, 8 - e)) % 2
         return remote(
             PG.at[zz(e), rows(half), pl.ds(own_col, CARRY)],
             XR.at[e, rows(half), :],
             gxs.at[e, half], gxr.at[e, half], along_x(1 - 2 * turn),
         )
 
-    def add_y(n, carry):
-        e = place(n)
+    def add_y(low):
+        e = place(low)
         for way in (0, 1):
             gy_copy(e, way).wait_recv()
         cols = pl.ds(give_col, SHARE)
@@ -337,12 +338,30 @@
 
         @pl.when(is_b)
         def _():
-            for half in (0, 1):
-                gx_copy(e, half).start()
-
-        return carry
-
-    def add_x(n, carry):
+            if not SPARE_X:
+                send = True
+            elif low == 0:
+                send = False
+                for half in (0, 1):
+                    gz_copy(half, half, 4).start()
+            else:
+                send = True
+                if low in (1, 2):
+                    half = 2 - low
+                    gz_copy(half, half, 4).wait_recv()
+                    span = rows(half)
+                    mid = pl.ds(own_col, CARRY)
+                    PG[zz(e), span, mid] = (
+                        PG[zz(e), span, mid].astype(F32) + ZR[half, 3, span, :].astype(F32)
+                    ).astype(BF)
+            if send:
+                for half in (0, 1):
+                    gx_copy(e, half).start()
+
+    def add_x(n):
+        if SPARE_X and n == 0:
+            return
+
         @pl.when(is_a)
         def _():
             e = place(n)
@@ -351,8 +370,6 @@
             cols = pl.ds(own_col, CARRY)
             PG[zz(e), :, cols] = (PG[zz(e), :, cols].astype(F32) + XR[e].astype(F32)).astype(BF)
 
-        return carry
-
     def gz_copy(way, half, reach):
         e = reach if way == 0 else 8 - reach
         return remote(
@@ -361,10 +378,10 @@
             gzs.at[way, half, reach - 1], gzr.at[way, half, reach - 1], along_z(1 - 2 * way),
         )
 
-    def serve_gz(reach):
+    def serve_gz(reach, halves=(0, 1)):
         @pl.when(is_a)
         def _():
-            for half in (0, 1):
+            for half in halves:
                 for way in (0, 1):
                     top = chain(way, half)
                     if reach > top:
@@ -385,30 +402,31 @@
     def owner(dy, dx):
         return (((y + dy) % 4) * 2 + (xh if dx == 0 else 1 - xh))
 
-    def f_copy(dy, dx):
+    def f_copy(dy, dx, half):
         slot = 2 * dy + dx
         size = 256 if dy % 2 == 0 else T
         return remote(
-            LB.at[owner(dy, dx), :, pl.ds(0, size)],
-            FR.at[slot, :, pl.ds(0, size)],
-            fs.at[slot], fr.at[slot], owner_device(dy, dx),
+            LB.at[owner(dy, dx), rows(half), pl.ds(0, size)],
+            FR.at[slot, rows(half), pl.ds(0, size)],
+            fs.at[slot, half], fr.at[slot, half], owner_device(dy, dx),
         )
 
-    def send_last():
+    def send_last(half):
+        span = rows(half)
         for j in range(8):
             u, shift = divmod(80 * j, T)
-            tile = PG[z, :, SHARE + u * T : SHARE + (u + 1) * T].astype(F32)
+            tile = PG[z, span, SHARE + u * T : SHARE + (u + 1) * T].astype(F32)
             if shift:
                 tile = pltpu.roll(tile, T - shift, 1)
             if shift + 80 > T:
-                more = PG[z, :, SHARE + (u + 1) * T : SHARE + (u + 2) * T].astype(F32)
-                tile = jnp.where(lanes(RP) < T - shift, tile, pltpu.roll(more, T - shift, 1))
-            LB[j, :, 0:T] = tile.astype(BF)
+                more = PG[z, span, SHARE + (u + 1) * T : SHARE + (u + 2) * T].astype(F32)
+                tile = jnp.where(lanes(SPAN[half][1]) < T - shift, tile, pltpu.roll(more, T - shift, 1))
+            LB[j, span, 0:T] = tile.astype(BF)
         for m in range(4):
             j = (m // 2) * 4 + m % 2 + 2 * par
-            LB[j, :, T : 2 * T] = PG[z, :, pl.ds(pl.multiple_of(par * CARRY + m * T, T), T)]
+            LB[j, span, T : 2 * T] = PG[z, span, pl.ds(pl.multiple_of(par * CARRY + m * T, T), T)]
         for dy, dx in turns:
-            f_copy(dy, dx).start()
+            f_copy(dy, dx, half).start()
 
     share = remote(SS, SR, cs.at[2], cr.at[2], sibling)
 
@@ -417,7 +435,8 @@
         rest = LB[me, :, 0:T].astype(F32)
         main = LB[me, :, T : 2 * T].astype(F32)
         for dy, dx in turns:
-            f_copy(dy, dx).wait_recv()
+            for half in (0, 1):
+                f_copy(dy, dx, half).wait_recv()
             rest = rest + FR[2 * dy + dx, :, 0:T].astype(F32)
             if dy % 2 == 0:
                 main = main + FR[2 * dy + dx, :, T : 2 * T].astype(F32)
@@ -518,15 +537,16 @@
         "YA": lambda n: serve_y(n, is_a),
         "YB": lambda n: serve_y(n, is_b),
         "part": lambda a, b: loop(a, b, partial_product),
-        "ay": lambda a, b: loop(a, b, add_y),
-        "ax": lambda a, b: loop(a, b, add_x),
+        "ay": lambda a, b: add_y(a),
+        "ax": lambda a, b: add_x(a),
         "gz": serve_gz,
         "zero": zero_grad,
         "E": lambda who, n: grad_in(who, GROUPS[n]),
         "G": lambda who, n: project(who, GROUPS[n]),
         "round": round_grad,
         "bwd": backward,
-        "last": lambda: pl.when(is_a)(send_last),
+        "gz0": lambda half: serve_gz(0, (half,)),
+        "last": lambda half: pl.when(is_a)(functools.partial(send_last, half)),
         "fin": lambda: pl.when(is_a)(finish),
     }
     for name, *args in PLAN:
@@ -559,14 +579,15 @@
 
     @pl.when(is_b)
     def _():
-        def sent_x(e, carry):
+        for e in range(8):
+            if SPARE_X and e == 4:
+                continue
             for half in (0, 1):
                 gx_copy(e, half).wait_send()
-            return carry
-
-        loop(0, 8, sent_x)
         for half in (0, 1):
             z_copy(half, half, 4).wait_send()
+            if SPARE_X:
+                gz_copy(half, half, 4).wait_send()
 
     @pl.when(is_a)
     def _():
@@ -579,7 +600,8 @@
                     z_copy(way, half, step).wait_send()
                     gz_copy(way, half, step).wait_send()
         for dy, dx in turns:
-            f_copy(dy, dx).wait_send()
+            for half in (0, 1):
+                f_copy(dy, dx, half).wait_send()
         share.wait_send()
 
 
@@ -635,7 +657,7 @@
             dma((8, 2)), dma((8, 2)),
             dma((8, 2)), dma((8, 2)),
             dma((2, 2, 4)), dma((2, 2, 4)),
-            dma((8,)), dma((8,)),
+            dma((8, 2)), dma((8, 2)),
             dma((3,)), dma((3,)),
         ],
         compiler_params=pltpu.CompilerParams(

time: 82.4 us -> 80.5 us (0.977)
  Pallas kernels: 81.5 us -> 79.6 us
    pallas_call x1, Pallas kernels: 79.4 us -> 77.5 us  [block_step(): pl.pallas_call(body_kernel, out_shape=tuple((V(*shape) for shape in shape...]
where the time goes in v4:
time: 80.5 us; the launch traced here: 80.4 us
  Pallas kernels  79.6 us (99%)
    pallas_call x1, Pallas kernels, block_step(): pl.pallas_call(body_kernel, out_shape=tuple((V(*shape) for shape in shape...  77.5 us
    pallas_call x1, Pallas kernels, block_step(): pl.pallas_call(store_kernel, out_shape=tuple((jax.ShapeDtypeStruct(*shape...  2.07 us

profile of v4, /device:TPU:1, one launch (start us, length us, event | category | flops | bytes accessed | tf_op | source)
XLA Modules:
  0.0 80.4 jit_solution(17135380821447118881)
XLA Ops:
  0.6 77.5 %shard_map.119 = (bf16[256,3200]{1,0:T(8,128)(2,1)S(1)}, bf16[256,1664]{1,0:T(8,128)(2,1)S(1)}, bf16[256,1664]{1,0:T(8,128)(2,1)S(1)}, bf16[256,1664]{1,0:T(8,128)(2,1)S(1)}, f32[200,104]{1,0:T(8,128)S(1)}) custom-call(s32[1,256]{1,0:T(1,128)} %seg_hbm.1, bf16[200,1664]{1,0:T(8,128)(2,1)} %codes_hbm.1, s32[52,200]{1,0:T(8,128)} %bitcast.1, ...), custom_call_target="tpu_custom_call" | custom-call | flops 10000000000 | bytes 20000000 | tf_op jit(solution)/shard_map/pallas_call | solution.py:625
  78.2 2.1 %shard_map.120 = (bf16[256,3200]{1,0:T(8,128)(2,1)}, bf16[256,1664]{1,0:T(8,128)(2,1)}, bf16[256,1664]{1,0:T(8,128)(2,1)}, bf16[256,1664]{1,0:T(8,128)(2,1)}, f32[200,104]{1,0:T(8,128)}) custom-call(bf16[256,3200]{1,0:T(8,128)(2,1)S(1)} %get-tuple-element.10.refs_0_, bf16[256,1664]{1,0:T(8,128)(2,1)S(1)} %get-tuple-element.11.refs_1_, ...), custom_call_target="tpu_custom_call" | custom-call | tf_op jit(solution)/shard_map/pallas_call | solution.py:669

commit v5 on v4

--- a/solution.py
+++ b/solution.py
@@ -29,20 +29,20 @@
 GROUPS = ((0,), (7, 1), (6, 2), (5, 3), (4,))
 
 PLAN = (
-    ("load", 6), ("load", 5), ("og", 0, 4), ("load", 4), ("og", 4, 8), ("load", 3), ("fwd", 0, 2), ("ogs",),
-    ("fwd", 2, 4), ("fwd", 4, 6), ("fwd", 6, 8), ("fwd", 8, 10), ("fwd", 10, 12), ("Z", 1), ("fwd", 12, 13), ("ord",),
-    ("ats",), ("X", 0), ("shares",), ("load", 7), ("part", 0, 1), ("X", 1), ("X", 2), ("Z", 2), ("Z", 3), ("YB", 0),
-    ("YA", 1), ("YA", 2), ("ay", 0, 1), ("YA", 3), ("part", 1, 2), ("YB", 1), ("Z", 4), ("X", 3), ("zero",),
-    ("ax", 0, 1), ("part", 2, 3), ("Z", 5), ("part", 3, 4), ("YB", 2), ("S", 0), ("gz", 4), ("ay", 1, 2), ("E", 0, 0),
-    ("S", 1), ("S", 2), ("Z", 6), ("S", 3), ("ay", 2, 3), ("YB", 3), ("part", 4, 5), ("YA", 4), ("ax", 1, 2),
-    ("part", 5, 6), ("ax", 2, 3), ("X", 4), ("G", 1, 0), ("gz", 3), ("X", 5), ("ay", 3, 4), ("ax", 3, 4), ("S", 4),
-    ("Z", 7), ("part", 6, 7), ("YA", 5), ("ay", 4, 5), ("E", 1, 1), ("YA", 6), ("E", 0, 1), ("X", 6), ("ax", 4, 5),
-    ("G", 0, 1), ("YB", 4), ("ay", 5, 6), ("gz", 2), ("part", 7, 8), ("G", 1, 2), ("ax", 5, 6), ("ay", 6, 7),
-    ("S", 5), ("YB", 5), ("YB", 6), ("G", 0, 2), ("YA", 7), ("S", 6), ("ax", 6, 7), ("gz", 1), ("X", 7), ("ay", 7, 8),
-    ("S", 7), ("G", 0, 3), ("YB", 7), ("E", 0, 4), ("ax", 7, 8), ("E", 0, 3), ("E", 1, 3), ("G", 1, 1), ("gz0", 0),
-    ("last", 0), ("G", 0, 4), ("E", 1, 0), ("E", 1, 4), ("gz0", 1), ("last", 1), ("E", 0, 2), ("G", 1, 3),
-    ("E", 1, 2), ("round",), ("bwd", 0, 2), ("bwd", 2, 4), ("G", 1, 4), ("bwd", 4, 6), ("bwd", 6, 8), ("bwd", 8, 10),
-    ("G", 0, 0), ("fin",), ("bwd", 10, 12), ("bwd", 12, 13),
+    ("load", 6), ("load", 5), ("load", 4), ("load", 3), ("og", 0, 4), ("fwd", 0, 2), ("og", 4, 8), ("fwd", 2, 4),
+    ("fwd", 4, 6), ("fwd", 6, 8), ("load", 7), ("fwd", 8, 10), ("ogs",), ("fwd", 10, 12), ("fwd", 12, 13), ("ord",),
+    ("ats",), ("Z", 1), ("X", 0), ("Z", 2), ("shares",), ("YB", 0), ("part", 0, 1), ("X", 1), ("part", 1, 2),
+    ("Z", 3), ("part", 2, 3), ("Z", 4), ("ay", 0, 1), ("YA", 1), ("part", 3, 4), ("Z", 5), ("part", 4, 5),
+    ("ax", 0, 1), ("YA", 2), ("X", 2), ("Z", 6), ("YA", 3), ("part", 5, 6), ("zero",), ("S", 0), ("gz", 4),
+    ("ay", 1, 2), ("part", 6, 7), ("ay", 2, 3), ("X", 3), ("E", 0, 0), ("X", 4), ("ax", 1, 2), ("ay", 3, 4),
+    ("YB", 1), ("part", 7, 8), ("X", 5), ("YA", 4), ("X", 6), ("ax", 2, 3), ("gz", 3), ("ax", 3, 4), ("ay", 4, 5),
+    ("S", 1), ("ax", 4, 5), ("gz", 2), ("ay", 5, 6), ("S", 2), ("ay", 6, 7), ("YB", 2), ("Z", 7), ("G", 1, 0),
+    ("YB", 3), ("S", 3), ("ax", 5, 6), ("E", 1, 0), ("ax", 6, 7), ("gz", 1), ("X", 7), ("YB", 4), ("ay", 7, 8),
+    ("G", 0, 1), ("YA", 5), ("ax", 7, 8), ("E", 0, 2), ("YB", 5), ("S", 4), ("YA", 6), ("G", 0, 0), ("YB", 6),
+    ("gz0", 0), ("YB", 7), ("YA", 7), ("E", 0, 3), ("S", 5), ("last", 0), ("G", 0, 3), ("G", 1, 1), ("E", 0, 4),
+    ("gz0", 1), ("S", 6), ("last", 1), ("S", 7), ("E", 1, 3), ("E", 1, 1), ("E", 0, 1), ("E", 1, 2), ("G", 0, 4),
+    ("G", 0, 2), ("G", 1, 2), ("E", 1, 4), ("round",), ("bwd", 0, 2), ("bwd", 2, 4), ("bwd", 4, 6), ("G", 1, 4),
+    ("bwd", 6, 8), ("fin",), ("G", 1, 3), ("bwd", 8, 10), ("bwd", 10, 12), ("bwd", 12, 13),
 )
 
 

time: 80.5 us -> 76.9 us (0.955)
  Pallas kernels: 79.6 us -> 76 us
    pallas_call x1, Pallas kernels: 77.5 us -> 73.9 us  [block_step(): pl.pallas_call(body_kernel, out_shape=tuple((V(*shape) for shape in shape...]
where the time goes in v5:
time: 76.9 us; the launch traced here: 76.8 us
  Pallas kernels  76 us (99%)
  between operations  0.8 us (1%)
    pallas_call x1, Pallas kernels, block_step(): pl.pallas_call(body_kernel, out_shape=tuple((V(*shape) for shape in shape...  73.9 us
    pallas_call x1, Pallas kernels, block_step(): pl.pallas_call(store_kernel, out_shape=tuple((jax.ShapeDtypeStruct(*shape...  2.07 us

profile of v5, /device:TPU:1, one launch (start us, length us, event | category | flops | bytes accessed | tf_op | source)
XLA Modules:
  0.0 76.8 jit_solution(10684994053602946379)
XLA Ops:
  0.6 73.9 %shard_map.119 = (bf16[256,3200]{1,0:T(8,128)(2,1)S(1)}, bf16[256,1664]{1,0:T(8,128)(2,1)S(1)}, bf16[256,1664]{1,0:T(8,128)(2,1)S(1)}, bf16[256,1664]{1,0:T(8,128)(2,1)S(1)}, f32[200,104]{1,0:T(8,128)S(1)}) custom-call(s32[1,256]{1,0:T(1,128)} %seg_hbm.1, bf16[200,1664]{1,0:T(8,128)(2,1)} %codes_hbm.1, s32[52,200]{1,0:T(8,128)} %bitcast.1, ...), custom_call_target="tpu_custom_call" | custom-call | flops 10000000000 | bytes 20000000 | tf_op jit(solution)/shard_map/pallas_call | solution.py:625
  74.6 2.1 %shard_map.120 = (bf16[256,3200]{1,0:T(8,128)(2,1)}, bf16[256,1664]{1,0:T(8,128)(2,1)}, bf16[256,1664]{1,0:T(8,128)(2,1)}, bf16[256,1664]{1,0:T(8,128)(2,1)}, f32[200,104]{1,0:T(8,128)}) custom-call(bf16[256,3200]{1,0:T(8,128)(2,1)S(1)} %get-tuple-element.10.refs_0_, bf16[256,1664]{1,0:T(8,128)(2,1)S(1)} %get-tuple-element.11.refs_1_, ...), custom_call_target="tpu_custom_call" | custom-call | tf_op jit(solution)/shard_map/pallas_call | solution.py:669

commit v6 on v5

--- a/solution.py
+++ b/solution.py
@@ -107,18 +107,15 @@
             ((codes_hbm, CODES), (exps_hbm, EXPS), (seg_hbm, SEG), (q_hbm, Q), (k_hbm, K), (v_hbm, V), (og_hbm, OG), (res_hbm, LO))
         )
     ]
-    for load in loads[:3]:
-        load.start()
+    for n in (1, 0, 2):
+        loads[n].start()
     barrier = pltpu.get_barrier_semaphore()
     greet = [along_z(1), along_z(-1), along_x(1), along_x(-1), along_y(1), along_y(-1), sibling]
     greet += [owner_device(2, 0), owner_device(0, 1), owner_device(1, 1), owner_device(2, 1), owner_device(3, 1)]
     for dev in greet:
         pl.semaphore_signal(barrier, inc=1, device_id=dev, device_id_type=MESH)
 
-    for load in loads[3:]:
-        load.start()
-    for load in loads[:3]:
-        load.wait()
+    loads[1].wait()
     exps = EXPS[...]
     scale = jnp.zeros(exps.shape, F32)
     for octave in range(-16, 1):
@@ -128,6 +125,10 @@
         == lax.broadcasted_iota(jnp.int32, (HD // BLOCK, HD), 0)
     ).astype(BF)
     wide = dot(scale.astype(BF), spread, 0, 0)
+    loads[0].wait()
+    for load in loads[3:]:
+        load.start()
+    loads[2].wait()
     block = CODES[...].astype(F32) * wide
     block = jnp.concatenate([block, jnp.zeros((RP - RB, HD), F32)], axis=0)
     W[xl * 8 + z] = block.astype(BF)

time: 76.9 us -> 76.9 us (level)
  no operation moved by 1% of the time
where the time goes in v6:
time: 76.9 us; the launch traced here: 76.8 us
  Pallas kernels  76 us (99%)
  between operations  0.8 us (1%)
    pallas_call x1, Pallas kernels, block_step(): pl.pallas_call(body_kernel, out_shape=tuple((V(*shape) for shape in shape...  73.9 us
    pallas_call x1, Pallas kernels, block_step(): pl.pallas_call(store_kernel, out_shape=tuple((jax.ShapeDtypeStruct(*shape...  2.07 us

profile of v6, /device:TPU:1, one launch (start us, length us, event | category | flops | bytes accessed | tf_op | source)
XLA Modules:
  0.0 76.8 jit_solution(13677930890419376644)
XLA Ops:
  0.6 73.9 %shard_map.119 = (bf16[256,3200]{1,0:T(8,128)(2,1)S(1)}, bf16[256,1664]{1,0:T(8,128)(2,1)S(1)}, bf16[256,1664]{1,0:T(8,128)(2,1)S(1)}, bf16[256,1664]{1,0:T(8,128)(2,1)S(1)}, f32[200,104]{1,0:T(8,128)S(1)}) custom-call(s32[1,256]{1,0:T(1,128)} %seg_hbm.1, bf16[200,1664]{1,0:T(8,128)(2,1)} %codes_hbm.1, s32[52,200]{1,0:T(8,128)} %bitcast.1, ...), custom_call_target="tpu_custom_call" | custom-call | flops 10000000000 | bytes 20000000 | tf_op jit(solution)/shard_map/pallas_call | solution.py:626
  74.5 2.1 %shard_map.120 = (bf16[256,3200]{1,0:T(8,128)(2,1)}, bf16[256,1664]{1,0:T(8,128)(2,1)}, bf16[256,1664]{1,0:T(8,128)(2,1)}, bf16[256,1664]{1,0:T(8,128)(2,1)}, f32[200,104]{1,0:T(8,128)}) custom-call(bf16[256,3200]{1,0:T(8,128)(2,1)S(1)} %get-tuple-element.10.refs_0_, bf16[256,1664]{1,0:T(8,128)(2,1)S(1)} %get-tuple-element.11.refs_1_, ...), custom_call_target="tpu_custom_call" | custom-call | tf_op jit(solution)/shard_map/pallas_call | solution.py:670
